TPU v7x, 256 devices: a whole 4x4x8 slice. The times are simulated.
256 devices in a mesh: tm: 8 (over z_lo, y), space: 32 (over z_hi, x, core).
Axes of the slice: x: 4, y: 4, z: 8 (z_hi: 4, z_lo: 2; z = z_hi * 2 + z_lo), core: 2. Of those that a mesh axis runs over, the one named last changes fastest.
Arguments:
- coupling: float32 [448, 65536], P(None, 'space'), may hold values from -0.02734375 to 0.02734375
- retain: float32 [65536], P('space'), may hold values from 0.5 to 0.92
- sources: float32 [96, 65536], P('tm', 'space'), may hold values from -1.5 to 1.5
- initial_guess: float32 [24, 65536], P('tm', 'space'), may hold values from -5 to 5
- start_field: float32 [65536], P('space'), may hold values from -5 to 5
- block_columns: int32 [1024, 6], P('space'), may hold values from 0 to 63
- send_lists: int32 [64, 16], P('space'), may hold values from 0 to 31, as said below
Outputs:
- point_values: float32 [24, 65536], P('tm', 'space')
- residual: float32 [24, 65536], P('tm', 'space')
Inputs may be any that keep to these rules, and one draw needn't show every extreme that they name: `block_columns`: entries are numbers in the extended list of the block's own space index: own blocks first, then the 16 blocks received from the lower neighbour, then the 16 from the upper one. `send_lists`: row 2 s lists the blocks that space index s sends to index s - 1, row 2 s + 1 those it sends to index s + 1, numbered within index s; the 16 entries of a row are distinct.
All inputs are finite; a program needn't handle non-finite values.
Results may differ from a plain program's by a relative error of at most 0.00015.
Values sent between devices are 32-bit elements; how exact they have to be, the bound alone decides.
A program may use at most 64 MiB of HBM per device.

v0:
```python
import jax
import jax.numpy as jnp
from jax import lax
from jax.sharding import PartitionSpec as P

BS = 64
STENCIL = 7
NBLK = 32
CF = 4
C_DEV = 3
PASSES = 2
HALO = 16


def with_halo(array, sides, width):
    for axis, dim in sides:
        devices, length = (lax.axis_size(axis), array.shape[dim])
        up = [(i, (i + 1) % devices) for i in range(devices - 1)]
        down = [(j, i) for i, j in up]
        last = lax.slice_in_dim(array, length - width, length, axis=dim)
        leading = lax.slice_in_dim(array, 0, width, axis=dim)
        before = lax.ppermute(last, axis, up)
        after = lax.ppermute(leading, axis, down)
        array = jnp.concatenate([before, array, after], axis=dim)
    return array


def shifted(value, axis, steps):
    count = lax.axis_size(axis)
    leading, last = (max(0, -steps), min(count, count - steps))
    return lax.ppermute(value, axis, [(source, source + steps) for source in range(leading, last)])


def neighbour_term(field_now, coupling, columns, flat_lists):
    count_rows = field_now.shape[0]
    blocks = field_now.reshape(count_rows, NBLK, BS)
    outgoing = blocks[:, flat_lists, :].reshape(count_rows, 2 * HALO * BS)
    widened = with_halo(outgoing, (("space", 1),), HALO * BS)
    from_lower = widened[:, : HALO * BS]
    from_upper = widened[:, 3 * HALO * BS :]
    extended = jnp.concatenate([field_now, from_lower, from_upper], axis=1).reshape(
        count_rows, NBLK + 2 * HALO, BS
    )
    picked = extended[:, columns, :].reshape(count_rows, NBLK, STENCIL * BS)
    weights = coupling.reshape(STENCIL * BS, NBLK, BS)
    result = jnp.einsum("rbi,ibc->rbc", picked, weights, precision=lax.Precision.HIGHEST)
    return result.reshape(count_rows, NBLK * BS)


def body(coupling, retain, sources, initial_guess, start_field, block_columns, send_lists):
    own_blocks = jnp.arange(NBLK, dtype=jnp.int32)[:, None]
    columns = jnp.concatenate([own_blocks, block_columns], axis=1)
    flat_lists = send_lists.reshape(2 * HALO)
    cell_count = retain.shape[0]
    forcing = sources.reshape(C_DEV, CF, cell_count)
    first_slice = lax.axis_index("tm") == 0
    start_row = start_field[None]

    def propagate(starting, forcing_rows):
        field_now = starting
        for section in range(CF):
            field_now = (
                retain[None] * field_now
                + neighbour_term(field_now, coupling, columns, flat_lists)
                + forcing_rows[:, section]
            )
        return field_now

    values = initial_guess
    for sweep_index in range(2 * PASSES):
        moved = shifted(values[C_DEV - 1 :], "tm", 1)
        moved = jnp.where(first_slice, start_row, moved)
        values = propagate(jnp.concatenate([moved, values[:-1]], axis=0), forcing)
    moved_last = shifted(values[C_DEV - 1 :], "tm", 1)
    moved_last = jnp.where(first_slice, start_row, moved_last)
    residual = propagate(jnp.concatenate([moved_last, values[:-1]], axis=0), forcing) - values
    return (values, residual)


def solution(mesh):
    placed = (
        P(None, "space"),
        P("space"),
        P("tm", "space"),
        P("tm", "space"),
        P("space"),
        P("space", None),
        P("space", None),
    )
    return jax.shard_map(
        body,
        mesh=mesh,
        in_specs=placed,
        out_specs=(P("tm", "space"), P("tm", "space")),
        check_vma=False,
    )
```

profile of v0, /device:TPU:103, one launch (start us, length us, event | category | flops | bytes accessed | tf_op | source)
XLA Modules:
  0.0 434.5 jit_solution(11923959383640648846)
XLA Ops:
  10.2 6.6 %collective-permute-start.1 = (f32[3,1024]{1,0:T(4,128)S(1)}, f32[3,1024]{1,0:T(4,128)S(1)}, u32[]{:S(2)}, u32[]{:S(2)}) collective-permute-start(f32[3,1024]{1,0:T(4,128)S(1)} %get-tuple-element.54), channel_id=1, source_target_pairs={{0,1},{1,2},{2,3},{3,4},{4,5},{5,6},{6,7},{7,8},{8,9},{9,10},{10,1... | collective-permute-start | bytes 36872 | tf_op jit(solution)/shard_map/ppermute | solution.py:22
  27.5 5.8 %copy_add_fusion.14 = (f32[3,32,64]{2,0,1:T(4,128)S(1)}, f32[3,32,64]{2,0,1:T(4,128)S(1)}) fusion(f32[3,32,64]{2,1,0:T(8,128)S(1)} %squeeze.15, f32[2,32,64]{2,0,1:T(2,128)S(1)} %copy.159, f32[1,32,64]{2,0,1:T(1,128)S(1)} %concatenate.148, f32[32,64]{1,0:T(8,128)S(1)} %mul.189, f32[448,32,64]{0,2,1:T(8,128)} %bitcast.205, f32[3,32,448]{2,1,0:T(8,128)S(1)} %reshape.580), kind=kOutput, calls=%fused_computation.114 | convolution fusion | flops 33054720 | bytes 3948544 | tf_op jit(solution)/shard_map/rbi,ibc->rbc/dot_general | solution.py:46
  34.1 6.3 %collective-permute-start.3 = (f32[3,1024]{1,0:T(4,128)S(1)}, f32[3,1024]{1,0:T(4,128)S(1)}, u32[]{:S(2)}, u32[]{:S(2)}) collective-permute-start(f32[3,1024]{1,0:T(4,128)S(1)} %get-tuple-element.52), channel_id=1, source_target_pairs={{0,1},{1,2},{2,3},{3,4},{4,5},{5,6},{6,7},{7,8},{8,9},{9,10},{10,1... | collective-permute-start | bytes 36872 | tf_op jit(solution)/shard_map/ppermute | solution.py:22
  42.4 7.3 %collective-permute-done.4 = f32[3,1024]{1,0:T(4,128)S(1)} collective-permute-done((f32[3,1024]{1,0:T(4,128)S(1)}, f32[3,1024]{1,0:T(4,128)S(1)}, u32[]{:S(2)}, u32[]{:S(2)}) %collective-permute-start.4) | collective-permute-done | bytes 12320 | tf_op jit(solution)/shard_map/ppermute | solution.py:23
  62.2 6.7 %collective-permute-done.6 = f32[3,1024]{1,0:T(4,128)S(1)} collective-permute-done((f32[3,1024]{1,0:T(4,128)S(1)}, f32[3,1024]{1,0:T(4,128)S(1)}, u32[]{:S(2)}, u32[]{:S(2)}) %collective-permute-start.6) | collective-permute-done | bytes 12320 | tf_op jit(solution)/shard_map/ppermute | solution.py:23
  81.2 6.8 %collective-permute-done.8 = f32[3,1024]{1,0:T(4,128)S(1)} collective-permute-done((f32[3,1024]{1,0:T(4,128)S(1)}, f32[3,1024]{1,0:T(4,128)S(1)}, u32[]{:S(2)}, u32[]{:S(2)}) %collective-permute-start.8) | collective-permute-done | bytes 12320 | tf_op jit(solution)/shard_map/ppermute | solution.py:23
  108.0 7.1 %collective-permute-done.11 = f32[3,1024]{1,0:T(4,128)S(1)} collective-permute-done((f32[3,1024]{1,0:T(4,128)S(1)}, f32[3,1024]{1,0:T(4,128)S(1)}, u32[]{:S(2)}, u32[]{:S(2)}) %collective-permute-start.11) | collective-permute-done | bytes 12320 | tf_op jit(solution)/shard_map/ppermute | solution.py:23
  116.5 5.8 %copy_add_fusion.13 = (f32[3,32,64]{2,0,1:T(4,128)S(1)}, f32[3,32,64]{2,0,1:T(4,128)S(1)}) fusion(f32[3,32,64]{2,1,0:T(8,128)S(1)} %squeeze.15, f32[2,32,64]{2,0,1:T(2,128)S(1)} %copy.187, f32[1,32,64]{2,0,1:T(1,128)S(1)} %concatenate.156, f32[32,64]{1,0:T(8,128)S(1)} %mul.189, f32[448,32,64]{0,2,1:T(8,128)} %bitcast.209, f32[3,32,448]{2,1,0:T(8,128)S(1)} %reshape.599), kind=kOutput, calls=%fused_computation.113 | convolution fusion | flops 33054720 | bytes 3948544 | tf_op jit(solution)/shard_map/rbi,ibc->rbc/dot_general | solution.py:46
  127.7 6.6 %collective-permute-done.13 = f32[3,1024]{1,0:T(4,128)S(1)} collective-permute-done((f32[3,1024]{1,0:T(4,128)S(1)}, f32[3,1024]{1,0:T(4,128)S(1)}, u32[]{:S(2)}, u32[]{:S(2)}) %collective-permute-start.13) | collective-permute-done | bytes 12320 | tf_op jit(solution)/shard_map/ppermute | solution.py:23
  146.7 6.8 %collective-permute-done.15 = f32[3,1024]{1,0:T(4,128)S(1)} collective-permute-done((f32[3,1024]{1,0:T(4,128)S(1)}, f32[3,1024]{1,0:T(4,128)S(1)}, u32[]{:S(2)}, u32[]{:S(2)}) %collective-permute-start.15) | collective-permute-done | bytes 12320 | tf_op jit(solution)/shard_map/ppermute | solution.py:23
  165.9 6.8 %collective-permute-done.17 = f32[3,1024]{1,0:T(4,128)S(1)} collective-permute-done((f32[3,1024]{1,0:T(4,128)S(1)}, f32[3,1024]{1,0:T(4,128)S(1)}, u32[]{:S(2)}, u32[]{:S(2)}) %collective-permute-start.17) | collective-permute-done | bytes 12320 | tf_op jit(solution)/shard_map/ppermute | solution.py:23
  193.1 6.7 %collective-permute-done.20 = f32[3,1024]{1,0:T(4,128)S(1)} collective-permute-done((f32[3,1024]{1,0:T(4,128)S(1)}, f32[3,1024]{1,0:T(4,128)S(1)}, u32[]{:S(2)}, u32[]{:S(2)}) %collective-permute-start.20) | collective-permute-done | bytes 12320 | tf_op jit(solution)/shard_map/ppermute | solution.py:23
  212.2 6.8 %collective-permute-done.22 = f32[3,1024]{1,0:T(4,128)S(1)} collective-permute-done((f32[3,1024]{1,0:T(4,128)S(1)}, f32[3,1024]{1,0:T(4,128)S(1)}, u32[]{:S(2)}, u32[]{:S(2)}) %collective-permute-start.22) | collective-permute-done | bytes 12320 | tf_op jit(solution)/shard_map/ppermute | solution.py:23
  231.4 6.8 %collective-permute-done.24 = f32[3,1024]{1,0:T(4,128)S(1)} collective-permute-done((f32[3,1024]{1,0:T(4,128)S(1)}, f32[3,1024]{1,0:T(4,128)S(1)}, u32[]{:S(2)}, u32[]{:S(2)}) %collective-permute-start.24) | collective-permute-done | bytes 12320 | tf_op jit(solution)/shard_map/ppermute | solution.py:23
  250.7 6.7 %collective-permute-done.26 = f32[3,1024]{1,0:T(4,128)S(1)} collective-permute-done((f32[3,1024]{1,0:T(4,128)S(1)}, f32[3,1024]{1,0:T(4,128)S(1)}, u32[]{:S(2)}, u32[]{:S(2)}) %collective-permute-start.26) | collective-permute-done | bytes 12320 | tf_op jit(solution)/shard_map/ppermute | solution.py:23
  277.4 7.1 %collective-permute-done.29 = f32[3,1024]{1,0:T(4,128)S(1)} collective-permute-done((f32[3,1024]{1,0:T(4,128)S(1)}, f32[3,1024]{1,0:T(4,128)S(1)}, u32[]{:S(2)}, u32[]{:S(2)}) %collective-permute-start.29) | collective-permute-done | bytes 12320 | tf_op jit(solution)/shard_map/ppermute | solution.py:23
  296.9 6.8 %collective-permute-done.31 = f32[3,1024]{1,0:T(4,128)S(1)} collective-permute-done((f32[3,1024]{1,0:T(4,128)S(1)}, f32[3,1024]{1,0:T(4,128)S(1)}, u32[]{:S(2)}, u32[]{:S(2)}) %collective-permute-start.31) | collective-permute-done | bytes 12320 | tf_op jit(solution)/shard_map/ppermute | solution.py:23
  316.3 6.6 %collective-permute-done.33 = f32[3,1024]{1,0:T(4,128)S(1)} collective-permute-done((f32[3,1024]{1,0:T(4,128)S(1)}, f32[3,1024]{1,0:T(4,128)S(1)}, u32[]{:S(2)}, u32[]{:S(2)}) %collective-permute-start.33) | collective-permute-done | bytes 12320 | tf_op jit(solution)/shard_map/ppermute | solution.py:23
  335.2 6.8 %collective-permute-done.35 = f32[3,1024]{1,0:T(4,128)S(1)} collective-permute-done((f32[3,1024]{1,0:T(4,128)S(1)}, f32[3,1024]{1,0:T(4,128)S(1)}, u32[]{:S(2)}, u32[]{:S(2)}) %collective-permute-start.35) | collective-permute-done | bytes 12320 | tf_op jit(solution)/shard_map/ppermute | solution.py:23
  362.1 7.1 %collective-permute-done.38 = f32[3,1024]{1,0:T(4,128)S(1)} collective-permute-done((f32[3,1024]{1,0:T(4,128)S(1)}, f32[3,1024]{1,0:T(4,128)S(1)}, u32[]{:S(2)}, u32[]{:S(2)}) %collective-permute-start.38) | collective-permute-done | bytes 12320 | tf_op jit(solution)/shard_map/ppermute | solution.py:23
  370.5 5.8 %copy_add_fusion.10 = (f32[3,32,64]{2,0,1:T(4,128)S(1)}, f32[3,32,64]{2,0,1:T(4,128)S(1)}) fusion(f32[3,32,64]{2,1,0:T(8,128)S(1)} %squeeze.15, f32[2,32,64]{2,0,1:T(2,128)S(1)} %copy.262, f32[1,32,64]{2,0,1:T(1,128)S(1)} %concatenate.180, f32[32,64]{1,0:T(8,128)S(1)} %mul.189, f32[448,32,64]{0,2,1:T(8,128)} %bitcast.221, f32[3,32,448]{2,1,0:T(8,128)S(1)} %reshape.650), kind=kOutput, calls=%fused_computation.110 | convolution fusion | flops 33054720 | bytes 3948544 | tf_op jit(solution)/shard_map/rbi,ibc->rbc/dot_general | solution.py:46
  381.8 6.6 %collective-permute-done.40 = f32[3,1024]{1,0:T(4,128)S(1)} collective-permute-done((f32[3,1024]{1,0:T(4,128)S(1)}, f32[3,1024]{1,0:T(4,128)S(1)}, u32[]{:S(2)}, u32[]{:S(2)}) %collective-permute-start.40) | collective-permute-done | bytes 12320 | tf_op jit(solution)/shard_map/ppermute | solution.py:23
  400.7 6.8 %collective-permute-done.42 = f32[3,1024]{1,0:T(4,128)S(1)} collective-permute-done((f32[3,1024]{1,0:T(4,128)S(1)}, f32[3,1024]{1,0:T(4,128)S(1)}, u32[]{:S(2)}, u32[]{:S(2)}) %collective-permute-start.42) | collective-permute-done | bytes 12320 | tf_op jit(solution)/shard_map/ppermute | solution.py:23
  419.9 6.8 %collective-permute-done.44 = f32[3,1024]{1,0:T(4,128)S(1)} collective-permute-done((f32[3,1024]{1,0:T(4,128)S(1)}, f32[3,1024]{1,0:T(4,128)S(1)}, u32[]{:S(2)}, u32[]{:S(2)}) %collective-permute-start.44) | collective-permute-done | bytes 12320 | tf_op jit(solution)/shard_map/ppermute | solution.py:23
  (416 shorter events, 271.2 us)
Async XLA Ops:
  1.4 6.7 %collective-permute-start = (f32[1,2048]{1,0:T(1,128)S(1)}, f32[1,2048]{1,0:T(1,128)S(1)}, u32[]{:S(2)}, u32[]{:S(2)}) collective-permute-start(f32[1,2048]{1,0:T(1,128)S(1)} %slice.178), channel_id=1, source_target_pairs={{0,32},{32,64},{64,96},{96,128},{128,160},{160,192},{192,224},{1,3... | collective-permute-start | bytes 24584 | tf_op jit(solution)/shard_map/ppermute | solution.py:31
  10.2 14.3 %collective-permute-start.1 = (f32[3,1024]{1,0:T(4,128)S(1)}, f32[3,1024]{1,0:T(4,128)S(1)}, u32[]{:S(2)}, u32[]{:S(2)}) collective-permute-start(f32[3,1024]{1,0:T(4,128)S(1)} %get-tuple-element.54), channel_id=1, source_target_pairs={{0,1},{1,2},{2,3},{3,4},{4,5},{5,6},{6,7},{7,8},{8,9},{9,10},{10,1... | collective-permute-start | bytes 36872 | tf_op jit(solution)/shard_map/ppermute | solution.py:22
  16.8 9.3 %collective-permute-start.2 = (f32[3,1024]{1,0:T(4,128)S(1)}, f32[3,1024]{1,0:T(4,128)S(1)}, u32[]{:S(2)}, u32[]{:S(2)}) collective-permute-start(f32[3,1024]{1,0:T(4,128)S(1)} %get-tuple-element.55), channel_id=1, source_target_pairs={{1,0},{2,1},{3,2},{4,3},{5,4},{6,5},{7,6},{8,7},{9,8},{10,9},{11,1... | collective-permute-start | bytes 36872 | tf_op jit(solution)/shard_map/ppermute | solution.py:23
  34.1 8.3 %collective-permute-start.3 = (f32[3,1024]{1,0:T(4,128)S(1)}, f32[3,1024]{1,0:T(4,128)S(1)}, u32[]{:S(2)}, u32[]{:S(2)}) collective-permute-start(f32[3,1024]{1,0:T(4,128)S(1)} %get-tuple-element.52), channel_id=1, source_target_pairs={{0,1},{1,2},{2,3},{3,4},{4,5},{5,6},{6,7},{7,8},{8,9},{9,10},{10,1... | collective-permute-start | bytes 36872 | tf_op jit(solution)/shard_map/ppermute | solution.py:22
  40.4 9.3 %collective-permute-start.4 = (f32[3,1024]{1,0:T(4,128)S(1)}, f32[3,1024]{1,0:T(4,128)S(1)}, u32[]{:S(2)}, u32[]{:S(2)}) collective-permute-start(f32[3,1024]{1,0:T(4,128)S(1)} %get-tuple-element.53), channel_id=1, source_target_pairs={{1,0},{2,1},{3,2},{4,3},{5,4},{6,5},{7,6},{8,7},{9,8},{10,9},{11,1... | collective-permute-start | bytes 36872 | tf_op jit(solution)/shard_map/ppermute | solution.py:23
  59.6 9.3 %collective-permute-start.6 = (f32[3,1024]{1,0:T(4,128)S(1)}, f32[3,1024]{1,0:T(4,128)S(1)}, u32[]{:S(2)}, u32[]{:S(2)}) collective-permute-start(f32[3,1024]{1,0:T(4,128)S(1)} %get-tuple-element.51), channel_id=1, source_target_pairs={{1,0},{2,1},{3,2},{4,3},{5,4},{6,5},{7,6},{8,7},{9,8},{10,9},{11,1... | collective-permute-start | bytes 36872 | tf_op jit(solution)/shard_map/ppermute | solution.py:23
  78.8 9.3 %collective-permute-start.8 = (f32[3,1024]{1,0:T(4,128)S(1)}, f32[3,1024]{1,0:T(4,128)S(1)}, u32[]{:S(2)}, u32[]{:S(2)}) collective-permute-start(f32[3,1024]{1,0:T(4,128)S(1)} %get-tuple-element.49), channel_id=1, source_target_pairs={{1,0},{2,1},{3,2},{4,3},{5,4},{6,5},{7,6},{8,7},{9,8},{10,9},{11,1... | collective-permute-start | bytes 36872 | tf_op jit(solution)/shard_map/ppermute | solution.py:23
  94.7 6.5 %collective-permute-start.9 = (f32[1,2048]{1,0:T(1,128)S(1)}, f32[1,2048]{1,0:T(1,128)S(1)}, u32[]{:S(2)}, u32[]{:S(2)}) collective-permute-start(f32[1,2048]{1,0:T(1,128)S(1)} %slice.324), channel_id=1, source_target_pairs={{0,32},{32,64},{64,96},{96,128},{128,160},{160,192},{192,224},{1,3... | collective-permute-start | bytes 24584 | tf_op jit(solution)/shard_map/ppermute | solution.py:31
  105.9 9.3 %collective-permute-start.11 = (f32[3,1024]{1,0:T(4,128)S(1)}, f32[3,1024]{1,0:T(4,128)S(1)}, u32[]{:S(2)}, u32[]{:S(2)}) collective-permute-start(f32[3,1024]{1,0:T(4,128)S(1)} %get-tuple-element.47), channel_id=1, source_target_pairs={{1,0},{2,1},{3,2},{4,3},{5,4},{6,5},{7,6},{8,7},{9,8},{10,9},{11,1... | collective-permute-start | bytes 36872 | tf_op jit(solution)/shard_map/ppermute | solution.py:23
  125.1 9.3 %collective-permute-start.13 = (f32[3,1024]{1,0:T(4,128)S(1)}, f32[3,1024]{1,0:T(4,128)S(1)}, u32[]{:S(2)}, u32[]{:S(2)}) collective-permute-start(f32[3,1024]{1,0:T(4,128)S(1)} %get-tuple-element.45), channel_id=1, source_target_pairs={{1,0},{2,1},{3,2},{4,3},{5,4},{6,5},{7,6},{8,7},{9,8},{10,9},{11,1... | collective-permute-start | bytes 36872 | tf_op jit(solution)/shard_map/ppermute | solution.py:23
  144.2 9.3 %collective-permute-start.15 = (f32[3,1024]{1,0:T(4,128)S(1)}, f32[3,1024]{1,0:T(4,128)S(1)}, u32[]{:S(2)}, u32[]{:S(2)}) collective-permute-start(f32[3,1024]{1,0:T(4,128)S(1)} %get-tuple-element.43), channel_id=1, source_target_pairs={{1,0},{2,1},{3,2},{4,3},{5,4},{6,5},{7,6},{8,7},{9,8},{10,9},{11,1... | collective-permute-start | bytes 36872 | tf_op jit(solution)/shard_map/ppermute | solution.py:23
  163.4 9.3 %collective-permute-start.17 = (f32[3,1024]{1,0:T(4,128)S(1)}, f32[3,1024]{1,0:T(4,128)S(1)}, u32[]{:S(2)}, u32[]{:S(2)}) collective-permute-start(f32[3,1024]{1,0:T(4,128)S(1)} %get-tuple-element.41), channel_id=1, source_target_pairs={{1,0},{2,1},{3,2},{4,3},{5,4},{6,5},{7,6},{8,7},{9,8},{10,9},{11,1... | collective-permute-start | bytes 36872 | tf_op jit(solution)/shard_map/ppermute | solution.py:23
  190.6 9.3 %collective-permute-start.20 = (f32[3,1024]{1,0:T(4,128)S(1)}, f32[3,1024]{1,0:T(4,128)S(1)}, u32[]{:S(2)}, u32[]{:S(2)}) collective-permute-start(f32[3,1024]{1,0:T(4,128)S(1)} %get-tuple-element.39), channel_id=1, source_target_pairs={{1,0},{2,1},{3,2},{4,3},{5,4},{6,5},{7,6},{8,7},{9,8},{10,9},{11,1... | collective-permute-start | bytes 36872 | tf_op jit(solution)/shard_map/ppermute | solution.py:23
  209.7 9.3 %collective-permute-start.22 = (f32[3,1024]{1,0:T(4,128)S(1)}, f32[3,1024]{1,0:T(4,128)S(1)}, u32[]{:S(2)}, u32[]{:S(2)}) collective-permute-start(f32[3,1024]{1,0:T(4,128)S(1)} %get-tuple-element.37), channel_id=1, source_target_pairs={{1,0},{2,1},{3,2},{4,3},{5,4},{6,5},{7,6},{8,7},{9,8},{10,9},{11,1... | collective-permute-start | bytes 36872 | tf_op jit(solution)/shard_map/ppermute | solution.py:23
  228.9 9.3 %collective-permute-start.24 = (f32[3,1024]{1,0:T(4,128)S(1)}, f32[3,1024]{1,0:T(4,128)S(1)}, u32[]{:S(2)}, u32[]{:S(2)}) collective-permute-start(f32[3,1024]{1,0:T(4,128)S(1)} %get-tuple-element.35), channel_id=1, source_target_pairs={{1,0},{2,1},{3,2},{4,3},{5,4},{6,5},{7,6},{8,7},{9,8},{10,9},{11,1... | collective-permute-start | bytes 36872 | tf_op jit(solution)/shard_map/ppermute | solution.py:23
  248.1 9.3 %collective-permute-start.26 = (f32[3,1024]{1,0:T(4,128)S(1)}, f32[3,1024]{1,0:T(4,128)S(1)}, u32[]{:S(2)}, u32[]{:S(2)}) collective-permute-start(f32[3,1024]{1,0:T(4,128)S(1)} %get-tuple-element.33), channel_id=1, source_target_pairs={{1,0},{2,1},{3,2},{4,3},{5,4},{6,5},{7,6},{8,7},{9,8},{10,9},{11,1... | collective-permute-start | bytes 36872 | tf_op jit(solution)/shard_map/ppermute | solution.py:23
  275.2 9.3 %collective-permute-start.29 = (f32[3,1024]{1,0:T(4,128)S(1)}, f32[3,1024]{1,0:T(4,128)S(1)}, u32[]{:S(2)}, u32[]{:S(2)}) collective-permute-start(f32[3,1024]{1,0:T(4,128)S(1)} %get-tuple-element.31), channel_id=1, source_target_pairs={{1,0},{2,1},{3,2},{4,3},{5,4},{6,5},{7,6},{8,7},{9,8},{10,9},{11,1... | collective-permute-start | bytes 36872 | tf_op jit(solution)/shard_map/ppermute | solution.py:23
  294.4 9.3 %collective-permute-start.31 = (f32[3,1024]{1,0:T(4,128)S(1)}, f32[3,1024]{1,0:T(4,128)S(1)}, u32[]{:S(2)}, u32[]{:S(2)}) collective-permute-start(f32[3,1024]{1,0:T(4,128)S(1)} %get-tuple-element.29), channel_id=1, source_target_pairs={{1,0},{2,1},{3,2},{4,3},{5,4},{6,5},{7,6},{8,7},{9,8},{10,9},{11,1... | collective-permute-start | bytes 36872 | tf_op jit(solution)/shard_map/ppermute | solution.py:23
  313.6 9.3 %collective-permute-start.33 = (f32[3,1024]{1,0:T(4,128)S(1)}, f32[3,1024]{1,0:T(4,128)S(1)}, u32[]{:S(2)}, u32[]{:S(2)}) collective-permute-start(f32[3,1024]{1,0:T(4,128)S(1)} %get-tuple-element.27), channel_id=1, source_target_pairs={{1,0},{2,1},{3,2},{4,3},{5,4},{6,5},{7,6},{8,7},{9,8},{10,9},{11,1... | collective-permute-start | bytes 36872 | tf_op jit(solution)/shard_map/ppermute | solution.py:23
  332.8 9.3 %collective-permute-start.35 = (f32[3,1024]{1,0:T(4,128)S(1)}, f32[3,1024]{1,0:T(4,128)S(1)}, u32[]{:S(2)}, u32[]{:S(2)}) collective-permute-start(f32[3,1024]{1,0:T(4,128)S(1)} %get-tuple-element.25), channel_id=1, source_target_pairs={{1,0},{2,1},{3,2},{4,3},{5,4},{6,5},{7,6},{8,7},{9,8},{10,9},{11,1... | collective-permute-start | bytes 36872 | tf_op jit(solution)/shard_map/ppermute | solution.py:23
  359.9 9.3 %collective-permute-start.38 = (f32[3,1024]{1,0:T(4,128)S(1)}, f32[3,1024]{1,0:T(4,128)S(1)}, u32[]{:S(2)}, u32[]{:S(2)}) collective-permute-start(f32[3,1024]{1,0:T(4,128)S(1)} %get-tuple-element.23), channel_id=1, source_target_pairs={{1,0},{2,1},{3,2},{4,3},{5,4},{6,5},{7,6},{8,7},{9,8},{10,9},{11,1... | collective-permute-start | bytes 36872 | tf_op jit(solution)/shard_map/ppermute | solution.py:23
  379.1 9.3 %collective-permute-start.40 = (f32[3,1024]{1,0:T(4,128)S(1)}, f32[3,1024]{1,0:T(4,128)S(1)}, u32[]{:S(2)}, u32[]{:S(2)}) collective-permute-start(f32[3,1024]{1,0:T(4,128)S(1)} %get-tuple-element.21), channel_id=1, source_target_pairs={{1,0},{2,1},{3,2},{4,3},{5,4},{6,5},{7,6},{8,7},{9,8},{10,9},{11,1... | collective-permute-start | bytes 36872 | tf_op jit(solution)/shard_map/ppermute | solution.py:23
  398.3 9.3 %collective-permute-start.42 = (f32[3,1024]{1,0:T(4,128)S(1)}, f32[3,1024]{1,0:T(4,128)S(1)}, u32[]{:S(2)}, u32[]{:S(2)}) collective-permute-start(f32[3,1024]{1,0:T(4,128)S(1)} %get-tuple-element.19), channel_id=1, source_target_pairs={{1,0},{2,1},{3,2},{4,3},{5,4},{6,5},{7,6},{8,7},{9,8},{10,9},{11,1... | collective-permute-start | bytes 36872 | tf_op jit(solution)/shard_map/ppermute | solution.py:23
  417.5 9.3 %collective-permute-start.44 = (f32[3,1024]{1,0:T(4,128)S(1)}, f32[3,1024]{1,0:T(4,128)S(1)}, u32[]{:S(2)}, u32[]{:S(2)}) collective-permute-start(f32[3,1024]{1,0:T(4,128)S(1)} %get-tuple-element.17), channel_id=1, source_target_pairs={{1,0},{2,1},{3,2},{4,3},{5,4},{6,5},{7,6},{8,7},{9,8},{10,9},{11,1... | collective-permute-start | bytes 36872 | tf_op jit(solution)/shard_map/ppermute | solution.py:23
  (24 other events, 227.7 us)
where the time goes:
time: 443 us; the launch traced here: 434 us
  waiting for transfers between devices  149 us (34%)
  matrix products  113 us (26%)
  starting transfers between devices  110 us (25%)
  local copies, waits for them, and re-layouts  53.5 us (12%)
  other arithmetic  5.77 us (1%)
    ppermute x20, waiting for transfers between devices, with_halo(): after = lax.ppermute(leading, axis, down)  132 us
    dot_general x20, matrix products, neighbour_term(): jnp.einsum('rbi,ibc->rbc', picked, weights, precision=lax.Precision.HIGHEST)  113 us
    ppermute x20, starting transfers between devices, with_halo(): before = lax.ppermute(last, axis, up)  52.3 us
    ppermute x20, starting transfers between devices, with_halo(): after = lax.ppermute(leading, axis, down)  46.5 us
    gather x40, local copies, waits for them, and re-layouts, neighbour_term(): picked = extended[:, columns, :].reshape(count_rows, NBLK, STENCIL * BS)  19.8 us
    ppermute x5, waiting for transfers between devices, shifted(): lax.ppermute(value, axis, [(source, source + steps) for source in range(l...  17.6 us
    gather x40, local copies, waits for them, and re-layouts, neighbour_term(): outgoing = blocks[:, flat_lists, :].reshape(count_rows, 2 * HALO * BS)  12.3 us
    ppermute x5, starting transfers between devices, shifted(): lax.ppermute(value, axis, [(source, source + steps) for source in range(l...  11.5 us
  transfers between devices with their start and end apart: 45, of which 24 were waited for; matrix products, arithmetic and copies ran while one was open for 2% of the time, Pallas kernels for 0%

commit v1 on v0

v1 whole, which is shorter than its diff:
```python
import functools

import jax
import jax.numpy as jnp
from jax import lax
from jax.experimental import pallas as pl
from jax.experimental.pallas import tpu as pltpu
from jax.sharding import PartitionSpec as P

BS = 64
STENCIL = 7
NBLK = 32
CF = 4
C_DEV = 3
SWEEPS = 5
HALO = 16
PAIRS = NBLK // 2
GROUPS = NBLK // 4
STEPS = SWEEPS * CF
REST = (STENCIL - 1) * BS
MESH = pl.DeviceIdType.MESH


def kernel(
    n_tm,
    n_space,
    columns,
    lists,
    coupling_hbm,
    retain,
    sources,
    guess,
    start,
    values_out,
    residual_out,
    coupling,
    own_weights,
    weights,
    forcing,
    guess_out,
    guess_in,
    retained,
    state,
    reached,
    doubled,
    parts,
    base,
    outbox,
    inbox,
    point_out,
    point_in,
    coupling_sem,
    send_sem,
    recv_sem,
    slice_send,
    slice_recv,
):
    tm, space = lax.axis_index("tm"), lax.axis_index("space")
    before = [lax.rem(tm + n_tm - d, n_tm) for d in range(3)]
    after = [lax.rem(tm + d, n_tm) for d in range(3)]
    has = (space > 0, space < n_space - 1)
    beside = (space - 1, space + 1)

    lane = lax.broadcasted_iota(jnp.int32, (8, 128), 1)
    row = lax.broadcasted_iota(jnp.int32, (8, 128), 0)
    low, top = lane < BS, row < 4
    field = lax.rem(row, 4)

    loads = [
        pltpu.make_async_copy(
            coupling_hbm.at[pl.ds(BS * k, BS), :], coupling.at[pl.ds(BS * k, BS), :], coupling_sem.at[k]
        )
        for k in range(STENCIL)
    ]
    for load in loads:
        load.start()

    def cells(p):
        return pl.ds(128 * p, 128)

    inbox[...] = jnp.zeros_like(inbox)
    for p in range(PAIRS):
        for f in range(C_DEV):
            guess_out[pl.ds(16 * f + p, 1), :] = guess[pl.ds(f, 1), cells(p)]
            forcing[pl.ds(64 * (4 + f) + 4 * p, 4), :] = sources[pl.ds(4 * f, 4), cells(p)]
    forcing[pl.ds(448, 64), :] = jnp.zeros((64, 128), jnp.float32)

    barrier = pltpu.get_barrier_semaphore()
    for other in (before[1], before[2], after[1], after[2]):
        pl.semaphore_signal(barrier, inc=1, device_id={"tm": other}, device_id_type=MESH)
    for side in range(2):

        @pl.when(has[side])
        def _():
            pl.semaphore_signal(barrier, inc=1, device_id={"space": beside[side]}, device_id_type=MESH)

    pl.semaphore_wait(barrier, 4 + has[0].astype(jnp.int32) + has[1].astype(jnp.int32))

    def to_slice(n, source, target, other):
        return pltpu.make_async_remote_copy(
            src_ref=source,
            dst_ref=target,
            send_sem=slice_send.at[n],
            recv_sem=slice_recv.at[n],
            device_id={"tm": other},
            device_id_type=MESH,
        )

    def interval(a):
        return forcing.at[pl.ds(64 * a, 64), :]

    slice_copies = [
        to_slice(0, guess_out.at[pl.ds(16, 32), :], guess_in.at[pl.ds(0, 32), :], after[2]),
        to_slice(1, guess_out.at[pl.ds(0, 16), :], guess_in.at[pl.ds(32, 16), :], after[1]),
        to_slice(2, interval(6), interval(0), after[2]),
        to_slice(3, interval(4), interval(1), after[1]),
        to_slice(4, interval(5), interval(2), after[1]),
        to_slice(5, interval(6), interval(3), after[1]),
    ]
    for copy in slice_copies:
        copy.start()
    point_copy = to_slice(6, point_out, point_in, before[1])

    def halo_copy(slot, side):
        return pltpu.make_async_remote_copy(
            src_ref=outbox.at[slot, side],
            dst_ref=inbox.at[slot, 1 - side],
            send_sem=send_sem.at[slot, side],
            recv_sem=recv_sem.at[slot, 1 - side],
            device_id={"space": beside[side]},
            device_id_type=MESH,
        )

    def twice(value):
        turned = pltpu.roll(value, BS, 1)
        return jnp.where(low, value, turned), jnp.where(low, turned, value)

    def in_parts(value):
        upper = value.astype(jnp.bfloat16).astype(jnp.float32)
        return jnp.where(top, upper, value - upper)

    def send(step, values):
        slot = lax.rem(step, 2)
        begins = jnp.where(lax.rem(step, CF) == 0, 4 - C_DEV * tm - step // CF, -1)
        for p in range(PAIRS):
            value = jnp.where(field == begins, start[pl.ds(p, 1), :], values[p])
            state[p] = value
            doubled[2 * p], doubled[2 * p + 1] = twice(value)
        for side in range(2):
            for q in range(HALO // 2):
                pair = jnp.where(low, doubled[lists[side, 2 * q]], doubled[lists[side, 2 * q + 1]])
                outbox[slot, side, pl.ds(4 * q, 4), :] = pair[:4]

            @pl.when(has[side])
            def _():
                halo_copy(slot, side).start()

    for copy in slice_copies[:2]:
        copy.wait_recv()
    first = []
    for p in range(PAIRS):
        rows = [guess_in[pl.ds(16 * f + p, 1), :] for f in range(C_DEV)]
        rows.append(jnp.zeros((1, 128), jnp.float32))
        first.append(jnp.concatenate(rows + rows, axis=0))
    send(jnp.int32(0), first)

    for p in range(PAIRS):
        retained[p] = jnp.where(top, retain[pl.ds(p, 1), :], 0.0)
    for k in range(STENCIL):
        loads[k].wait()
        target, at, gap = (own_weights, 0, BS) if k == 0 else (weights, BS * (k - 1), REST)

        @pl.loop(0, BS // 16)
        def _(n, k=k, target=target, at=at, gap=gap):
            entries = coupling[pl.ds(pl.multiple_of(BS * k + 16 * n, 16), 16), :]
            upper = entries.astype(jnp.bfloat16)
            target[pl.ds(pl.multiple_of(at + 16 * n, 16), 16), :] = upper
            target[pl.ds(pl.multiple_of(at + gap + 16 * n, 16), 16), :] = (
                entries - upper.astype(jnp.float32)
            ).astype(jnp.bfloat16)

    def on_diagonal(product):
        return [
            jnp.where(
                low,
                product[16 * h : 16 * h + 8, 128 * h : 128 * h + 128],
                product[16 * h + 8 : 16 * h + 16, 128 * h : 128 * h + 128],
            )
            for h in range(2)
        ]

    def one_step(step, carry):
        slot = lax.rem(step, 2)

        @pl.when(step == 0)
        def _():
            for copy in slice_copies[2:]:
                copy.wait_recv()

        @pl.when(step == 4 * CF)
        def _():
            for p in range(PAIRS):
                value = reached[p]
                values_out[pl.ds(0, 2), cells(p)] = value[1:3]
                point_out[pl.ds(p, 1), :] = value[0:1]
            point_copy.start()

        at = (step // CF) * 64 + lax.rem(step, CF)
        for g in range(GROUPS):
            own = []
            for b in range(4 * g, 4 * g + 4):
                own.append(in_parts(doubled[b]))
                parts[b] = own[-1]
            product = jnp.dot(
                jnp.concatenate(own, axis=0).astype(jnp.bfloat16),
                own_weights[:, 256 * g : 256 * g + 256],
                preferred_element_type=jnp.float32,
            )
            for h, pair in enumerate(on_diagonal(product)):
                p = 2 * g + h
                heat = forcing[pl.ds(at + 4 * p, 4, stride=64), :]
                heat = jnp.concatenate([heat, jnp.zeros((4, 128), jnp.float32)], axis=0)
                base[p] = pair + retained[p] * state[p] + heat

        for side in range(2):

            @pl.when(has[side])
            def _():
                halo_copy(slot, 1 - side).wait_recv()

        for side in range(2):
            for q in range(HALO // 2):
                value = inbox[slot, side, pl.ds(4 * q, 4), :]
                both = twice(in_parts(jnp.concatenate([value, value], axis=0)))
                n = NBLK + HALO * side + 2 * q
                parts[n], parts[n + 1] = both

        values = []
        for g in range(GROUPS):
            picked = []
            for b in range(4 * g, 4 * g + 4):
                picked.append(
                    jnp.concatenate(
                        [
                            jnp.where(low, parts[columns[b, k]], parts[columns[b, k + 1]])
                            for k in range(0, STENCIL - 1, 2)
                        ],
                        axis=1,
                    )
                )
            left = jnp.concatenate(picked, axis=0).astype(jnp.bfloat16)
            product = jnp.dot(
                jnp.concatenate([left, left], axis=1),
                weights[:, 256 * g : 256 * g + 256],
                preferred_element_type=jnp.float32,
            )
            for h, pair in enumerate(on_diagonal(product)):
                total = base[2 * g + h] + pair
                values.append(total + pltpu.roll(total, 4, 0))
                reached[2 * g + h] = values[-1]

        for side in range(2):

            @pl.when(has[side])
            def _():
                halo_copy(slot, side).wait_send()

        @pl.when(step < STEPS - 1)
        def _():
            send(step + 1, [reached[p] for p in range(PAIRS)])

        return carry

    lax.fori_loop(0, STEPS, one_step, 0)

    for copy in slice_copies:
        copy.wait_send()
    point_copy.wait()
    for p in range(PAIRS):
        values_out[pl.ds(2, 1), cells(p)] = point_in[pl.ds(p, 1), :]
        residual_out[:, cells(p)] = reached[p][:3] - values_out[:, cells(p)]


def body(n_tm, n_space, coupling, retain, sources, initial_guess, start_field, block_columns, send_lists):
    count = retain.shape[0]
    f32, bf16 = jnp.float32, jnp.bfloat16
    smem, vmem = (pl.BlockSpec(memory_space=space) for space in (pltpu.SMEM, pltpu.VMEM))
    return pl.pallas_call(
        functools.partial(kernel, n_tm, n_space),
        out_shape=(jax.ShapeDtypeStruct((C_DEV, count), f32),) * 2,
        in_specs=[smem, smem, pl.BlockSpec(memory_space=pl.ANY), vmem, vmem, vmem, vmem],
        out_specs=(vmem, vmem),
        scratch_shapes=[
            pltpu.VMEM((STENCIL * BS, count), f32),
            pltpu.VMEM((2 * BS, count), bf16),
            pltpu.VMEM((2 * REST, count), bf16),
            pltpu.VMEM((512, 128), f32),
            pltpu.VMEM((48, 128), f32),
            pltpu.VMEM((48, 128), f32),
            pltpu.VMEM((PAIRS, 8, 128), f32),
            pltpu.VMEM((PAIRS, 8, 128), f32),
            pltpu.VMEM((PAIRS, 8, 128), f32),
            pltpu.VMEM((NBLK, 8, 128), f32),
            pltpu.VMEM((NBLK + 2 * HALO, 8, 128), f32),
            pltpu.VMEM((PAIRS, 8, 128), f32),
            pltpu.VMEM((2, 2, 32, 128), f32),
            pltpu.VMEM((2, 2, 32, 128), f32),
            pltpu.VMEM((16, 128), f32),
            pltpu.VMEM((16, 128), f32),
            pltpu.SemaphoreType.DMA((STENCIL,)),
            pltpu.SemaphoreType.DMA((2, 2)),
            pltpu.SemaphoreType.DMA((2, 2)),
            pltpu.SemaphoreType.DMA((7,)),
            pltpu.SemaphoreType.DMA((7,)),
        ],
        compiler_params=pltpu.CompilerParams(
            collective_id=0, has_side_effects=True, vmem_limit_bytes=32 * 2**20
        ),
    )(
        block_columns,
        send_lists,
        coupling,
        retain.reshape(PAIRS, 128),
        sources,
        initial_guess,
        start_field.reshape(PAIRS, 128),
    )


def solution(mesh):
    placed = (
        P(None, "space"),
        P("space"),
        P("tm", "space"),
        P("tm", "space"),
        P("space"),
        P("space", None),
        P("space", None),
    )
    return jax.shard_map(
        functools.partial(body, mesh.shape["tm"], mesh.shape["space"]),
        mesh=mesh,
        in_specs=placed,
        out_specs=(P("tm", "space"), P("tm", "space")),
        check_vma=False,
    )
```

time: 443 us -> 124 us (0.28)
  the two profiles are of different devices: /device:TPU:103 before, /device:TPU:71 now
where the time goes in v1:
time: 124 us
  Pallas kernels  116 us (94%)
  local copies, waits for them, and re-layouts  7.77 us (6%)
    pallas_call x1, Pallas kernels, body(): pl.pallas_call(functools.partial(kernel, n_tm, n_space), out_shape=(jax.S...  116 us
    unnamed x15, local copies, waits for them, and re-layouts  7.77 us

profile of v1, /device:TPU:71, one launch (start us, length us, event | category | flops | bytes accessed | tf_op | source)
XLA Modules:
  0.0 124.1 jit_solution(11745547835515254444)
XLA Ops:
  0.6 0.8 copy.9.columns
  1.4 0.0 copy-start
  1.4 2.0 %copy-done = f32[448,2048]{1,0:T(8,128)S(1)} copy-done((f32[448,2048]{1,0:T(8,128)S(1)}, f32[448,2048]{1,0:T(8,128)}, u32[]{:S(2)}) %copy-start) | copy-done | bytes 3670040
  3.4 0.0 copy-start.1
  3.4 0.9 copy-done.1
  4.3 0.0 copy-start.2
  4.3 0.8 copy-done.2
  5.1 0.0 copy-start.3
  5.1 0.7 copy-done.3
  5.8 0.0 copy-start.4
  5.8 0.7 copy-done.4
  6.5 0.0 copy-start.5
  6.5 0.7 copy-done.5
  7.2 115.7 %shard_map.86 = (f32[3,2048]{1,0:T(4,128)S(1)}, f32[3,2048]{1,0:T(4,128)S(1)}) custom-call(s32[32,6]{1,0:T(8,128)S(1)} %copy.9.columns, s32[2,16]{1,0:T(2,128)S(1)} %copy-done.5, f32[448,2048]{1,0:T(8,128)S(1)} %copy-done, f32[16,128]{1,0:T(8,128)S(1)} %bitcast.2, f32[12,2048]{1,0:T(8,128)S(1)} %copy-done.1, f32[3,2048]{1,0:T(4,128)S(1)} %copy-done.2, ...), custom_call_target="tpu_custom_call" | custom-call | tf_op jit(solution)/shard_map/pallas_call | solution.py:288
  122.9 0.6 copy.12
  123.5 0.6 copy.13
Async XLA Ops:
  1.4 2.0 %copy-start = (f32[448,2048]{1,0:T(8,128)S(1)}, f32[448,2048]{1,0:T(8,128)}, u32[]{:S(2)}) copy-start(f32[448,2048]{1,0:T(8,128)} %coupling_hbm.1) | copy-start | bytes 11010052
  3.4 0.9 copy-start.1
  4.3 0.8 copy-start.2
  5.1 0.7 copy-start.3
  5.8 0.7 copy-start.4
  6.5 0.7 copy-start.5

commit v2 on v1

--- a/solution.py
+++ b/solution.py
@@ -27,12 +27,16 @@
     columns,
     lists,
     coupling_hbm,
+    retain_hbm,
+    sources_hbm,
+    guess_hbm,
+    start_hbm,
+    values_out,
+    residual_out,
     retain,
     sources,
     guess,
     start,
-    values_out,
-    residual_out,
     coupling,
     own_weights,
     weights,
@@ -50,6 +54,7 @@
     point_out,
     point_in,
     coupling_sem,
+    input_sem,
     send_sem,
     recv_sem,
     slice_send,
@@ -72,27 +77,35 @@
         )
         for k in range(STENCIL)
     ]
-    for load in loads:
+    inputs = [
+        pltpu.make_async_copy(source, target, input_sem.at[n])
+        for n, (source, target) in enumerate(
+            ((guess_hbm, guess), (sources_hbm, sources), (start_hbm, start), (retain_hbm, retain))
+        )
+    ]
+    for load in inputs + loads:
         load.start()
 
     def cells(p):
         return pl.ds(128 * p, 128)
 
     inbox[...] = jnp.zeros_like(inbox)
+    barrier = pltpu.get_barrier_semaphore()
+    for other in (before[1], before[2], after[1], after[2]):
+        pl.semaphore_signal(barrier, inc=1, device_id={"tm": other}, device_id_type=MESH)
+    for side in range(2):
+
+        @pl.when(has[side])
+        def _():
+            pl.semaphore_signal(barrier, inc=1, device_id={"space": beside[side]}, device_id_type=MESH)
+
+    for load in inputs[:2]:
+        load.wait()
     for p in range(PAIRS):
         for f in range(C_DEV):
             guess_out[pl.ds(16 * f + p, 1), :] = guess[pl.ds(f, 1), cells(p)]
             forcing[pl.ds(64 * (4 + f) + 4 * p, 4), :] = sources[pl.ds(4 * f, 4), cells(p)]
     forcing[pl.ds(448, 64), :] = jnp.zeros((64, 128), jnp.float32)
-
-    barrier = pltpu.get_barrier_semaphore()
-    for other in (before[1], before[2], after[1], after[2]):
-        pl.semaphore_signal(barrier, inc=1, device_id={"tm": other}, device_id_type=MESH)
-    for side in range(2):
-
-        @pl.when(has[side])
-        def _():
-            pl.semaphore_signal(barrier, inc=1, device_id={"space": beside[side]}, device_id_type=MESH)
 
     pl.semaphore_wait(barrier, 4 + has[0].astype(jnp.int32) + has[1].astype(jnp.int32))
 
@@ -157,6 +170,7 @@
 
     for copy in slice_copies[:2]:
         copy.wait_recv()
+    inputs[2].wait()
     first = []
     for p in range(PAIRS):
         rows = [guess_in[pl.ds(16 * f + p, 1), :] for f in range(C_DEV)]
@@ -164,6 +178,7 @@
         first.append(jnp.concatenate(rows + rows, axis=0))
     send(jnp.int32(0), first)
 
+    inputs[3].wait()
     for p in range(PAIRS):
         retained[p] = jnp.where(top, retain[pl.ds(p, 1), :], 0.0)
     for k in range(STENCIL):
@@ -242,7 +257,7 @@
                 picked.append(
                     jnp.concatenate(
                         [
-                            jnp.where(low, parts[columns[b, k]], parts[columns[b, k + 1]])
+                            jnp.where(low, parts[columns[k, b]], parts[columns[k + 1, b]])
                             for k in range(0, STENCIL - 1, 2)
                         ],
                         axis=1,
@@ -288,9 +303,13 @@
     return pl.pallas_call(
         functools.partial(kernel, n_tm, n_space),
         out_shape=(jax.ShapeDtypeStruct((C_DEV, count), f32),) * 2,
-        in_specs=[smem, smem, pl.BlockSpec(memory_space=pl.ANY), vmem, vmem, vmem, vmem],
+        in_specs=[smem, smem] + [pl.BlockSpec(memory_space=pl.ANY)] * 5,
         out_specs=(vmem, vmem),
         scratch_shapes=[
+            pltpu.VMEM((PAIRS, 128), f32),
+            pltpu.VMEM((C_DEV * CF, count), f32),
+            pltpu.VMEM((C_DEV, count), f32),
+            pltpu.VMEM((PAIRS, 128), f32),
             pltpu.VMEM((STENCIL * BS, count), f32),
             pltpu.VMEM((2 * BS, count), bf16),
             pltpu.VMEM((2 * REST, count), bf16),
@@ -308,16 +327,17 @@
             pltpu.VMEM((16, 128), f32),
             pltpu.VMEM((16, 128), f32),
             pltpu.SemaphoreType.DMA((STENCIL,)),
+            pltpu.SemaphoreType.DMA((4,)),
             pltpu.SemaphoreType.DMA((2, 2)),
             pltpu.SemaphoreType.DMA((2, 2)),
             pltpu.SemaphoreType.DMA((7,)),
             pltpu.SemaphoreType.DMA((7,)),
         ],
         compiler_params=pltpu.CompilerParams(
-            collective_id=0, has_side_effects=True, vmem_limit_bytes=32 * 2**20
+            collective_id=0, has_side_effects=True, vmem_limit_bytes=60 * 2**20
         ),
     )(
-        block_columns,
+        block_columns.T,
         send_lists,
         coupling,
         retain.reshape(PAIRS, 128),

time: 124 us -> 120 us (0.968)
  local copies, waits for them, and re-layouts: 7.77 us -> 2.76 us
    unnamed x15 -> x2, local copies, waits for them, and re-layouts: 7.77 us -> 2.76 us
where the time goes in v2:
time: 120 us
  Pallas kernels  116 us (97%)
  local copies, waits for them, and re-layouts  2.76 us (2%)
    pallas_call x1, Pallas kernels, body(): pl.pallas_call(functools.partial(kernel, n_tm, n_space), out_shape=(jax.S...  116 us
    unnamed x2, local copies, waits for them, and re-layouts  2.76 us

profile of v2, /device:TPU:71, one launch (start us, length us, event | category | flops | bytes accessed | tf_op | source)
XLA Modules:
  0.0 119.7 jit_solution(11681485793544853909)
XLA Ops:
  0.6 116.3 %shard_map.86 = (f32[3,2048]{1,0:T(4,128)}, f32[3,2048]{1,0:T(4,128)}) custom-call(s32[6,32]{1,0:T(8,128)} %bitcast.5, s32[2,16]{1,0:T(2,128)} %lists.1, f32[448,2048]{1,0:T(8,128)} %coupling_hbm.1, f32[16,128]{1,0:T(8,128)} %bitcast.3, f32[12,2048]{1,0:T(8,128)} %sources_hbm.1, f32[3,2048]{1,0:T(4,128)} %guess_hbm.1, f32[16,128]{1,0:T(8,128)} %bitcast.4), custom_call_target="tpu_custom_call" | custom-call | tf_op jit(solution)/shard_map/pallas_call | solution.py:303
  117.0 1.4 %copy.11 = f32[3,2048]{1,0:T(4,128)} copy(f32[3,2048]{1,0:T(4,128)} %get-tuple-element.4) | data formatting | bytes 49152
  118.4 1.4 %copy.12 = f32[3,2048]{1,0:T(4,128)} copy(f32[3,2048]{1,0:T(4,128)} %get-tuple-element.5) | data formatting | bytes 49152

commit v3 on v2

--- a/solution.py
+++ b/solution.py
@@ -18,6 +18,9 @@
 GROUPS = NBLK // 4
 STEPS = SWEEPS * CF
 REST = (STENCIL - 1) * BS
+ROW = 8
+SPREAD = 2
+AHEAD = 5
 MESH = pl.DeviceIdType.MESH
 
 
@@ -31,6 +34,7 @@
     sources_hbm,
     guess_hbm,
     start_hbm,
+    columns_hbm,
     values_out,
     residual_out,
     retain,
@@ -53,18 +57,52 @@
     inbox,
     point_out,
     point_in,
+    piece,
+    far_coupling,
+    far_weights,
+    far_forcing_out,
+    far_forcing,
+    far_cells_out,
+    far_cells,
+    columns_own,
+    far_slots_out,
+    far_slots_in,
+    far_slots,
+    block_rows,
+    block_forcing,
+    block_cells,
+    far_out,
+    far_in,
+    relay_in,
+    far_parts,
     coupling_sem,
     input_sem,
     send_sem,
     recv_sem,
     slice_send,
     slice_recv,
+    far_send,
+    far_recv,
+    spread_send,
+    spread_recv,
+    field_send,
+    field_recv,
+    relay_send,
+    relay_recv,
 ):
     tm, space = lax.axis_index("tm"), lax.axis_index("space")
     before = [lax.rem(tm + n_tm - d, n_tm) for d in range(3)]
     after = [lax.rem(tm + d, n_tm) for d in range(3)]
     has = (space > 0, space < n_space - 1)
     beside = (space - 1, space + 1)
+    place = lax.rem(space, ROW)
+    across = ((place == 0) & has[0], (place == ROW - 1) & has[1])
+    is_far = across[0] | across[1]
+    is_relay = ((place == 1) & (space > 1)) | ((place == ROW - 2) & (space < n_space - 2))
+    upper_half = (place >= ROW // 2).astype(jnp.int32)
+    partner = space + 2 * upper_half - 1
+    second = space + 4 * upper_half - 2
+    rows_each = STENCIL * BS // n_tm
 
     lane = lax.broadcasted_iota(jnp.int32, (8, 128), 1)
     row = lax.broadcasted_iota(jnp.int32, (8, 128), 0)
@@ -80,7 +118,7 @@
     inputs = [
         pltpu.make_async_copy(source, target, input_sem.at[n])
         for n, (source, target) in enumerate(
-            ((guess_hbm, guess), (sources_hbm, sources), (start_hbm, start), (retain_hbm, retain))
+            ((guess_hbm, guess), (sources_hbm, sources), (start_hbm, start), (retain_hbm, retain), (columns_hbm, columns_own))
         )
     ]
     for load in inputs + loads:
@@ -98,6 +136,17 @@
         @pl.when(has[side])
         def _():
             pl.semaphore_signal(barrier, inc=1, device_id={"space": beside[side]}, device_id_type=MESH)
+
+    @pl.when(is_far)
+    def _():
+        for d in range(3, n_tm - 2):
+            pl.semaphore_signal(
+                barrier, inc=1, device_id={"tm": lax.rem(tm + d, n_tm)}, device_id_type=MESH
+            )
+
+    @pl.when(is_far | is_relay)
+    def _():
+        pl.semaphore_signal(barrier, inc=1, device_id={"space": second}, device_id_type=MESH)
 
     for load in inputs[:2]:
         load.wait()
@@ -107,7 +156,14 @@
             forcing[pl.ds(64 * (4 + f) + 4 * p, 4), :] = sources[pl.ds(4 * f, 4), cells(p)]
     forcing[pl.ds(448, 64), :] = jnp.zeros((64, 128), jnp.float32)
 
-    pl.semaphore_wait(barrier, 4 + has[0].astype(jnp.int32) + has[1].astype(jnp.int32))
+    pl.semaphore_wait(
+        barrier,
+        4
+        + has[0].astype(jnp.int32)
+        + has[1].astype(jnp.int32)
+        + (n_tm - 5) * is_far.astype(jnp.int32)
+        + (is_far | is_relay).astype(jnp.int32),
+    )
 
     def to_slice(n, source, target, other):
         return pltpu.make_async_remote_copy(
@@ -152,21 +208,99 @@
         upper = value.astype(jnp.bfloat16).astype(jnp.float32)
         return jnp.where(top, upper, value - upper)
 
+    def to_partner(n, source, target):
+        return pltpu.make_async_remote_copy(
+            src_ref=source,
+            dst_ref=target,
+            send_sem=far_send.at[n],
+            recv_sem=far_recv.at[n],
+            device_id={"space": partner},
+            device_id_type=MESH,
+        )
+
+    def rows_of(slice_at):
+        return far_coupling.at[pl.ds(pl.multiple_of(rows_each * slice_at, 8), rows_each), :]
+
+    far_copies = [
+        to_partner(0, piece, rows_of(tm)),
+        to_partner(1, far_forcing_out, far_forcing),
+        to_partner(2, far_cells_out, far_cells),
+        to_partner(3, far_slots_out, far_slots_in),
+    ]
+
+    def spread_copy(d, slice_at):
+        return pltpu.make_async_remote_copy(
+            src_ref=rows_of(slice_at),
+            dst_ref=rows_of(slice_at),
+            send_sem=spread_send.at[d],
+            recv_sem=spread_recv.at[d],
+            device_id={"tm": lax.rem(tm + d, n_tm)},
+            device_id_type=MESH,
+        )
+
+    def field_copy(step):
+        slot = lax.rem(step, 2)
+        return pltpu.make_async_remote_copy(
+            src_ref=far_out.at[slot],
+            dst_ref=far_in.at[step],
+            send_sem=field_send.at[slot],
+            recv_sem=field_recv.at[step],
+            device_id={"space": partner},
+            device_id_type=MESH,
+        )
+
+    def relay_copy(step):
+        slot = lax.rem(step, 2)
+        return pltpu.make_async_remote_copy(
+            src_ref=outbox.at[slot, upper_half],
+            dst_ref=relay_in.at[step],
+            send_sem=relay_send.at[slot],
+            recv_sem=relay_recv.at[step],
+            device_id={"space": second},
+            device_id_type=MESH,
+        )
+
+    def near(step, side):
+        return has[side] & jnp.logical_not(across[side] & (step >= AHEAD))
+
+    def fields_go(step):
+        return (step >= AHEAD - 1) & (step < STEPS - 1)
+
+    def store_twice(target, p, rows, value):
+        half = lax.broadcasted_iota(jnp.int32, value.shape, 1) < BS
+        turned = pltpu.roll(value, BS, 1)
+        target[2 * p, rows, :] = jnp.where(half, value, turned)
+        target[2 * p + 1, rows, :] = jnp.where(half, turned, value)
+
+    def of_listed(blocks, q):
+        values = [blocks[lists[upper_half, 2 * q + h]] for h in range(2)]
+        return jnp.where(lax.broadcasted_iota(jnp.int32, values[0].shape, 1) < BS, *values)
+
     def send(step, values):
         slot = lax.rem(step, 2)
         begins = jnp.where(lax.rem(step, CF) == 0, 4 - C_DEV * tm - step // CF, -1)
         for p in range(PAIRS):
             value = jnp.where(field == begins, start[pl.ds(p, 1), :], values[p])
             state[p] = value
+            far_out[slot, pl.ds(4 * p, 4), :] = value[:4]
             doubled[2 * p], doubled[2 * p + 1] = twice(value)
+
+        @pl.when(is_far & fields_go(step))
+        def _():
+            field_copy(step).start()
+
         for side in range(2):
             for q in range(HALO // 2):
                 pair = jnp.where(low, doubled[lists[side, 2 * q]], doubled[lists[side, 2 * q + 1]])
                 outbox[slot, side, pl.ds(4 * q, 4), :] = pair[:4]
 
-            @pl.when(has[side])
+            @pl.when(near(step, side))
             def _():
                 halo_copy(slot, side).start()
+
+        @pl.when(is_relay & fields_go(step))
+        def _():
+            relay_copy(step).start()
 
     for copy in slice_copies[:2]:
         copy.wait_recv()
@@ -179,10 +313,22 @@
     send(jnp.int32(0), first)
 
     inputs[3].wait()
+    inputs[4].wait()
     for p in range(PAIRS):
         retained[p] = jnp.where(top, retain[pl.ds(p, 1), :], 0.0)
+    for load in loads:
+        load.wait()
+
+    @pl.when(is_far)
+    def _():
+        for p in range(PAIRS):
+            own_rows = pl.ds(pl.multiple_of(rows_each * tm, 8), rows_each)
+            store_twice(block_rows, p, pl.ds(0, rows_each), coupling[own_rows, cells(p)])
+        for q in range(HALO // 2):
+            piece[:, cells(q)] = of_listed(block_rows, q)
+        far_copies[0].start()
+
     for k in range(STENCIL):
-        loads[k].wait()
         target, at, gap = (own_weights, 0, BS) if k == 0 else (weights, BS * (k - 1), REST)
 
         @pl.loop(0, BS // 16)
@@ -204,6 +350,49 @@
             for h in range(2)
         ]
 
+    def four_rows(value):
+        return twice(in_parts(jnp.concatenate([value, value], axis=0)))
+
+    def listed_by_partner(step):
+        slot = lax.rem(step, 2)
+        field_copy(step).wait_recv()
+        relay_copy(step).wait_recv()
+        for p in range(PAIRS):
+            far_parts[2 * p], far_parts[2 * p + 1] = four_rows(far_in[step, pl.ds(4 * p, 4), :])
+        for q in range(HALO // 2):
+            at = NBLK + HALO * upper_half + 2 * q
+            far_parts[at], far_parts[at + 1] = four_rows(relay_in[step, pl.ds(4 * q, 4), :])
+            at = NBLK + HALO * (1 - upper_half) + 2 * q
+            far_parts[at], far_parts[at + 1] = four_rows(outbox[slot, upper_half, pl.ds(4 * q, 4), :])
+        begins = jnp.where(lax.rem(step + 1, CF) == 0, 4 - C_DEV * tm - (step + 1) // CF, -1)
+        for g in range(HALO // 4):
+            picked, firsts = [], []
+            for j in range(4 * g, 4 * g + 4):
+                firsts.append(far_parts[far_slots[j, STENCIL - 1]])
+                rest = [
+                    jnp.where(
+                        low,
+                        far_parts[far_slots[j, k]],
+                        far_parts[far_slots[j, k + 1]],
+                    )
+                    for k in range(0, STENCIL - 1, 2)
+                ]
+                picked.append(jnp.concatenate(rest + rest + firsts[-1:], axis=1))
+            product = jnp.dot(
+                jnp.concatenate(picked, axis=0).astype(jnp.bfloat16),
+                far_weights[:, 256 * g : 256 * g + 256],
+                preferred_element_type=jnp.float32,
+            )
+            for h, pair in enumerate(on_diagonal(product)):
+                q = 2 * g + h
+                heat = far_forcing[pl.ds(step + 32 * q, 4, stride=CF), :]
+                heat = jnp.concatenate([heat, jnp.zeros((4, 128), jnp.float32)], axis=0)
+                now = jnp.where(low, firsts[2 * h], firsts[2 * h + 1])
+                total = pair + far_cells[pl.ds(q, 1), :] * now + heat
+                value = total + pltpu.roll(total, 4, 0)
+                value = jnp.where(field == begins, far_cells[pl.ds(8 + q, 1), :], value)
+                inbox[1 - slot, upper_half, pl.ds(4 * q, 4), :] = value[:4]
+
     def one_step(step, carry):
         slot = lax.rem(step, 2)
 
@@ -211,6 +400,62 @@
         def _():
             for copy in slice_copies[2:]:
                 copy.wait_recv()
+
+        @pl.when((step == 0) & is_far)
+        def _():
+            for p in range(PAIRS):
+                for a in range(8):
+                    store_twice(block_forcing, p, pl.ds(4 * a, 4), forcing[pl.ds(64 * a + 4 * p, 4), :])
+                for n, source in enumerate((retain, start)):
+                    store_twice(block_cells, p, pl.ds(n, 1), source[pl.ds(p, 1), :])
+            for q in range(HALO // 2):
+                far_forcing_out[pl.ds(32 * q, 32), :] = of_listed(block_forcing, q)
+                both = of_listed(block_cells, q)
+                far_cells_out[pl.ds(q, 1), :] = both[0:1]
+                far_cells_out[pl.ds(8 + q, 1), :] = both[1:2]
+            wide = lax.broadcasted_iota(jnp.int32, (HALO, NBLK), 0)
+            listed = jnp.zeros((HALO, NBLK), jnp.int32)
+            for j in range(HALO):
+                listed = jnp.where(wide == j, lists[upper_half, j], listed)
+            chosen = listed == lax.broadcasted_iota(jnp.int32, (HALO, NBLK), 1)
+            place_at = lax.broadcasted_iota(jnp.int32, (HALO, 128), 1)
+            table = jnp.zeros((HALO, 128), jnp.int32)
+            for k in range(STENCIL):
+                if k < STENCIL - 1:
+                    found = jnp.where(chosen, columns_own[pl.ds(k, 1), :], 0)
+                else:
+                    found = jnp.where(chosen, listed, 0)
+                table = jnp.where(place_at == k, jnp.sum(found, axis=1, keepdims=True), table)
+            far_slots_out[...] = table
+            for copy in far_copies[1:]:
+                copy.start()
+
+        @pl.when((step == SPREAD) & is_far)
+        def _():
+            far_copies[0].wait_recv()
+            for d in range(1, n_tm):
+                spread_copy(d, tm).start()
+
+        @pl.when((step == AHEAD - 1) & is_far)
+        def _():
+            for copy in far_copies[1:]:
+                copy.wait_recv()
+            slots = pltpu.make_async_copy(far_slots_in, far_slots, input_sem.at[5])
+            slots.start()
+            slots.wait()
+            for d in range(1, n_tm):
+                spread_copy(d, lax.rem(tm + n_tm - d, n_tm)).wait_recv()
+            for k in range(STENCIL):
+                at, gap = (2 * REST, BS) if k == 0 else (BS * (k - 1), REST)
+
+                @pl.loop(0, BS // 16)
+                def _(n, k=k, at=at, gap=gap):
+                    entries = far_coupling[pl.ds(pl.multiple_of(BS * k + 16 * n, 16), 16), :]
+                    upper = entries.astype(jnp.bfloat16)
+                    far_weights[pl.ds(pl.multiple_of(at + 16 * n, 16), 16), :] = upper
+                    far_weights[pl.ds(pl.multiple_of(at + gap + 16 * n, 16), 16), :] = (
+                        entries - upper.astype(jnp.float32)
+                    ).astype(jnp.bfloat16)
 
         @pl.when(step == 4 * CF)
         def _():
@@ -237,18 +482,21 @@
                 heat = jnp.concatenate([heat, jnp.zeros((4, 128), jnp.float32)], axis=0)
                 base[p] = pair + retained[p] * state[p] + heat
 
+        @pl.when(is_far & (step >= AHEAD))
+        def _():
+            listed_by_partner(step - 1)
+
         for side in range(2):
 
-            @pl.when(has[side])
+            @pl.when(near(step, side))
             def _():
                 halo_copy(slot, 1 - side).wait_recv()
 
         for side in range(2):
             for q in range(HALO // 2):
                 value = inbox[slot, side, pl.ds(4 * q, 4), :]
-                both = twice(in_parts(jnp.concatenate([value, value], axis=0)))
                 n = NBLK + HALO * side + 2 * q
-                parts[n], parts[n + 1] = both
+                parts[n], parts[n + 1] = four_rows(value)
 
         values = []
         for g in range(GROUPS):
@@ -276,10 +524,18 @@
 
         for side in range(2):
 
-            @pl.when(has[side])
+            @pl.when(near(step, side))
             def _():
                 halo_copy(slot, side).wait_send()
 
+        @pl.when(is_far & fields_go(step))
+        def _():
+            field_copy(step).wait_send()
+
+        @pl.when(is_relay & fields_go(step))
+        def _():
+            relay_copy(step).wait_send()
+
         @pl.when(step < STEPS - 1)
         def _():
             send(step + 1, [reached[p] for p in range(PAIRS)])
@@ -290,6 +546,14 @@
 
     for copy in slice_copies:
         copy.wait_send()
+
+    @pl.when(is_far)
+    def _():
+        for copy in far_copies:
+            copy.wait_send()
+        for d in range(1, n_tm):
+            spread_copy(d, tm).wait_send()
+
     point_copy.wait()
     for p in range(PAIRS):
         values_out[pl.ds(2, 1), cells(p)] = point_in[pl.ds(p, 1), :]
@@ -303,7 +567,7 @@
     return pl.pallas_call(
         functools.partial(kernel, n_tm, n_space),
         out_shape=(jax.ShapeDtypeStruct((C_DEV, count), f32),) * 2,
-        in_specs=[smem, smem] + [pl.BlockSpec(memory_space=pl.ANY)] * 5,
+        in_specs=[smem, smem] + [pl.BlockSpec(memory_space=pl.ANY)] * 6,
         out_specs=(vmem, vmem),
         scratch_shapes=[
             pltpu.VMEM((PAIRS, 128), f32),
@@ -326,12 +590,38 @@
             pltpu.VMEM((2, 2, 32, 128), f32),
             pltpu.VMEM((16, 128), f32),
             pltpu.VMEM((16, 128), f32),
+            pltpu.VMEM((STENCIL * BS // n_tm, count // 2), f32),
+            pltpu.VMEM((STENCIL * BS, count // 2), f32),
+            pltpu.VMEM((2 * STENCIL * BS, count // 2), bf16),
+            pltpu.VMEM((256, 128), f32),
+            pltpu.VMEM((256, 128), f32),
+            pltpu.VMEM((16, 128), f32),
+            pltpu.VMEM((16, 128), f32),
+            pltpu.VMEM((STENCIL - 1, NBLK), jnp.int32),
+            pltpu.VMEM((HALO, 128), jnp.int32),
+            pltpu.VMEM((HALO, 128), jnp.int32),
+            pltpu.SMEM((HALO, 128), jnp.int32),
+            pltpu.VMEM((NBLK, STENCIL * BS // n_tm, 128), f32),
+            pltpu.VMEM((NBLK, 32, 128), f32),
+            pltpu.VMEM((NBLK, 8, 128), f32),
+            pltpu.VMEM((2, 64, 128), f32),
+            pltpu.VMEM((STEPS, 64, 128), f32),
+            pltpu.VMEM((STEPS, 32, 128), f32),
+            pltpu.VMEM((NBLK + 2 * HALO, 8, 128), f32),
             pltpu.SemaphoreType.DMA((STENCIL,)),
-            pltpu.SemaphoreType.DMA((4,)),
+            pltpu.SemaphoreType.DMA((6,)),
             pltpu.SemaphoreType.DMA((2, 2)),
             pltpu.SemaphoreType.DMA((2, 2)),
             pltpu.SemaphoreType.DMA((7,)),
             pltpu.SemaphoreType.DMA((7,)),
+            pltpu.SemaphoreType.DMA((4,)),
+            pltpu.SemaphoreType.DMA((4,)),
+            pltpu.SemaphoreType.DMA((n_tm,)),
+            pltpu.SemaphoreType.DMA((n_tm,)),
+            pltpu.SemaphoreType.DMA((2,)),
+            pltpu.SemaphoreType.DMA((STEPS,)),
+            pltpu.SemaphoreType.DMA((2,)),
+            pltpu.SemaphoreType.DMA((STEPS,)),
         ],
         compiler_params=pltpu.CompilerParams(
             collective_id=0, has_side_effects=True, vmem_limit_bytes=60 * 2**20
@@ -344,6 +634,7 @@
         sources,
         initial_guess,
         start_field.reshape(PAIRS, 128),
+        block_columns.T,
     )
 
 

time: 120 us -> 98.9 us (0.82)
  Pallas kernels: 116 us -> 95.2 us
    pallas_call x1, Pallas kernels: 116 us -> 95.2 us  [body(): pl.pallas_call(functools.partial(kernel, n_tm, n_space), out_shape=(jax.S...]
where the time goes in v3:
time: 98.9 us; the launch traced here: 98.6 us
  Pallas kernels  95.2 us (96%)
  local copies, waits for them, and re-layouts  2.76 us (3%)
    pallas_call x1, Pallas kernels, body(): pl.pallas_call(functools.partial(kernel, n_tm, n_space), out_shape=(jax.S...  95.2 us
    unnamed x2, local copies, waits for them, and re-layouts  2.76 us

profile of v3, /device:TPU:71, one launch (start us, length us, event | category | flops | bytes accessed | tf_op | source)
XLA Modules:
  0.0 98.6 jit_solution(17614488291150143695)
XLA Ops:
  0.6 95.2 %shard_map.86 = (f32[3,2048]{1,0:T(4,128)}, f32[3,2048]{1,0:T(4,128)}) custom-call(s32[6,32]{1,0:T(8,128)} %bitcast.3, s32[2,16]{1,0:T(2,128)} %lists.1, f32[448,2048]{1,0:T(8,128)} %coupling_hbm.1, f32[16,128]{1,0:T(8,128)} %bitcast.5, f32[12,2048]{1,0:T(8,128)} %sources_hbm.1, f32[3,2048]{1,0:T(4,128)} %guess_hbm.1, f32[16,128]{1,0:T(8,128)} %bitcast.6, ...), custom_call_target="tpu_custom_call" | custom-call | tf_op jit(solution)/shard_map/pallas_call | solution.py:567
  95.9 1.4 %copy.11 = f32[3,2048]{1,0:T(4,128)} copy(f32[3,2048]{1,0:T(4,128)} %get-tuple-element.4) | data formatting | bytes 49152
  97.3 1.4 %copy.12 = f32[3,2048]{1,0:T(4,128)} copy(f32[3,2048]{1,0:T(4,128)} %get-tuple-element.5) | data formatting | bytes 49152

commit v4 on v3

--- a/solution.py
+++ b/solution.py
@@ -19,8 +19,8 @@
 STEPS = SWEEPS * CF
 REST = (STENCIL - 1) * BS
 ROW = 8
-SPREAD = 2
-AHEAD = 5
+SPREAD = 1
+AHEAD = 4
 MESH = pl.DeviceIdType.MESH
 
 
@@ -156,15 +156,6 @@
             forcing[pl.ds(64 * (4 + f) + 4 * p, 4), :] = sources[pl.ds(4 * f, 4), cells(p)]
     forcing[pl.ds(448, 64), :] = jnp.zeros((64, 128), jnp.float32)
 
-    pl.semaphore_wait(
-        barrier,
-        4
-        + has[0].astype(jnp.int32)
-        + has[1].astype(jnp.int32)
-        + (n_tm - 5) * is_far.astype(jnp.int32)
-        + (is_far | is_relay).astype(jnp.int32),
-    )
-
     def to_slice(n, source, target, other):
         return pltpu.make_async_remote_copy(
             src_ref=source,
@@ -186,8 +177,6 @@
         to_slice(4, interval(5), interval(2), after[1]),
         to_slice(5, interval(6), interval(3), after[1]),
     ]
-    for copy in slice_copies:
-        copy.start()
     point_copy = to_slice(6, point_out, point_in, before[1])
 
     def halo_copy(slot, side):
@@ -302,6 +291,35 @@
         def _():
             relay_copy(step).start()
 
+    @pl.when(is_far)
+    def _():
+        for load in loads:
+            load.wait()
+        for p in range(PAIRS):
+            own_rows = pl.ds(pl.multiple_of(rows_each * tm, 8), rows_each)
+            store_twice(block_rows, p, pl.ds(0, rows_each), coupling[own_rows, cells(p)])
+        for q in range(HALO // 2):
+            piece[:, cells(q)] = of_listed(block_rows, q)
+
+    pl.semaphore_wait(
+        barrier,
+        4
+        + has[0].astype(jnp.int32)
+        + has[1].astype(jnp.int32)
+        + (n_tm - 5) * is_far.astype(jnp.int32)
+        + (is_far | is_relay).astype(jnp.int32),
+    )
+
+
+    for copy in slice_copies[:2]:
+        copy.start()
+
+    @pl.when(is_far)
+    def _():
+        far_copies[0].start()
+
+    for copy in slice_copies[2:]:
+        copy.start()
     for copy in slice_copies[:2]:
         copy.wait_recv()
     inputs[2].wait()
@@ -316,17 +334,10 @@
     inputs[4].wait()
     for p in range(PAIRS):
         retained[p] = jnp.where(top, retain[pl.ds(p, 1), :], 0.0)
-    for load in loads:
-        load.wait()
-
-    @pl.when(is_far)
+    @pl.when(jnp.logical_not(is_far))
     def _():
-        for p in range(PAIRS):
-            own_rows = pl.ds(pl.multiple_of(rows_each * tm, 8), rows_each)
-            store_twice(block_rows, p, pl.ds(0, rows_each), coupling[own_rows, cells(p)])
-        for q in range(HALO // 2):
-            piece[:, cells(q)] = of_listed(block_rows, q)
-        far_copies[0].start()
+        for load in loads:
+            load.wait()
 
     for k in range(STENCIL):
         target, at, gap = (own_weights, 0, BS) if k == 0 else (weights, BS * (k - 1), REST)

time: 98.9 us -> 94.4 us (0.954); the launches traced: 98.6 us -> 92.8 us
  Pallas kernels: 95.2 us -> 89.4 us
    pallas_call x1, Pallas kernels: 95.2 us -> 89.4 us  [body(): pl.pallas_call(functools.partial(kernel, n_tm, n_space), out_shape=(jax.S...]
where the time goes in v4:
time: 94.4 us; the launch traced here: 92.8 us
  Pallas kernels  89.4 us (95%)
  local copies, waits for them, and re-layouts  2.76 us (3%)
    pallas_call x1, Pallas kernels, body(): pl.pallas_call(functools.partial(kernel, n_tm, n_space), out_shape=(jax.S...  89.4 us
    unnamed x2, local copies, waits for them, and re-layouts  2.76 us

profile of v4, /device:TPU:71, one launch (start us, length us, event | category | flops | bytes accessed | tf_op | source)
XLA Modules:
  0.0 92.8 jit_solution(8990442485583905222)
XLA Ops:
  0.6 89.4 %shard_map.86 = (f32[3,2048]{1,0:T(4,128)}, f32[3,2048]{1,0:T(4,128)}) custom-call(s32[6,32]{1,0:T(8,128)} %bitcast.3, s32[2,16]{1,0:T(2,128)} %lists.1, f32[448,2048]{1,0:T(8,128)} %coupling_hbm.1, f32[16,128]{1,0:T(8,128)} %bitcast.5, f32[12,2048]{1,0:T(8,128)} %sources_hbm.1, f32[3,2048]{1,0:T(4,128)} %guess_hbm.1, f32[16,128]{1,0:T(8,128)} %bitcast.6, ...), custom_call_target="tpu_custom_call" | custom-call | tf_op jit(solution)/shard_map/pallas_call | solution.py:578
  90.1 1.4 %copy.11 = f32[3,2048]{1,0:T(4,128)} copy(f32[3,2048]{1,0:T(4,128)} %get-tuple-element.4) | data formatting | bytes 49152
  91.4 1.4 %copy.12 = f32[3,2048]{1,0:T(4,128)} copy(f32[3,2048]{1,0:T(4,128)} %get-tuple-element.5) | data formatting | bytes 49152

commit v5 on v4

--- a/solution.py
+++ b/solution.py
@@ -27,8 +27,7 @@
 def kernel(
     n_tm,
     n_space,
-    columns,
-    lists,
+    lists_hbm,
     coupling_hbm,
     retain_hbm,
     sources_hbm,
@@ -37,6 +36,8 @@
     columns_hbm,
     values_out,
     residual_out,
+    columns,
+    lists,
     retain,
     sources,
     guess,
@@ -103,6 +104,7 @@
     partner = space + 2 * upper_half - 1
     second = space + 4 * upper_half - 2
     rows_each = STENCIL * BS // n_tm
+    cross = lax.rem(space, 2)
 
     lane = lax.broadcasted_iota(jnp.int32, (8, 128), 1)
     row = lax.broadcasted_iota(jnp.int32, (8, 128), 0)
@@ -118,7 +120,7 @@
     inputs = [
         pltpu.make_async_copy(source, target, input_sem.at[n])
         for n, (source, target) in enumerate(
-            ((guess_hbm, guess), (sources_hbm, sources), (start_hbm, start), (retain_hbm, retain), (columns_hbm, columns_own))
+            ((guess_hbm, guess), (sources_hbm, sources), (start_hbm, start), (retain_hbm, retain), (columns_hbm, columns_own), (columns_hbm, columns), (lists_hbm, lists))
         )
     ]
     for load in inputs + loads:
@@ -148,7 +150,7 @@
     def _():
         pl.semaphore_signal(barrier, inc=1, device_id={"space": second}, device_id_type=MESH)
 
-    for load in inputs[:2]:
+    for load in inputs[:2] + inputs[5:]:
         load.wait()
     for p in range(PAIRS):
         for f in range(C_DEV):
@@ -185,7 +187,7 @@
             dst_ref=inbox.at[slot, 1 - side],
             send_sem=send_sem.at[slot, side],
             recv_sem=recv_sem.at[slot, 1 - side],
-            device_id={"space": beside[side]},
+            device_id={"space": space + 2 * side - 1},
             device_id_type=MESH,
         )
 
@@ -250,7 +252,9 @@
         )
 
     def near(step, side):
-        return has[side] & jnp.logical_not(across[side] & (step >= AHEAD))
+        lower = has[0] & jnp.logical_not(across[0] & (step >= AHEAD))
+        upper = has[1] & jnp.logical_not(across[1] & (step >= AHEAD))
+        return ((side == 0) & lower) | ((side == 1) & upper)
 
     def fields_go(step):
         return (step >= AHEAD - 1) & (step < STEPS - 1)
@@ -265,20 +269,21 @@
         values = [blocks[lists[upper_half, 2 * q + h]] for h in range(2)]
         return jnp.where(lax.broadcasted_iota(jnp.int32, values[0].shape, 1) < BS, *values)
 
-    def send(step, values):
+    def arrive(step, p, value):
+        begins = jnp.where(lax.rem(step, CF) == 0, 4 - C_DEV * tm - step // CF, -1)
+        value = jnp.where(field == begins, start[pl.ds(p, 1), :], value)
+        state[p] = value
+        far_out[lax.rem(step, 2), pl.ds(4 * p, 4), :] = value[:4]
+        doubled[2 * p], doubled[2 * p + 1] = twice(value)
+
+    def send(step):
         slot = lax.rem(step, 2)
-        begins = jnp.where(lax.rem(step, CF) == 0, 4 - C_DEV * tm - step // CF, -1)
-        for p in range(PAIRS):
-            value = jnp.where(field == begins, start[pl.ds(p, 1), :], values[p])
-            state[p] = value
-            far_out[slot, pl.ds(4 * p, 4), :] = value[:4]
-            doubled[2 * p], doubled[2 * p + 1] = twice(value)
 
         @pl.when(is_far & fields_go(step))
         def _():
             field_copy(step).start()
 
-        for side in range(2):
+        for side in (cross, 1 - cross):
             for q in range(HALO // 2):
                 pair = jnp.where(low, doubled[lists[side, 2 * q]], doubled[lists[side, 2 * q + 1]])
                 outbox[slot, side, pl.ds(4 * q, 4), :] = pair[:4]
@@ -323,12 +328,11 @@
     for copy in slice_copies[:2]:
         copy.wait_recv()
     inputs[2].wait()
-    first = []
     for p in range(PAIRS):
         rows = [guess_in[pl.ds(16 * f + p, 1), :] for f in range(C_DEV)]
         rows.append(jnp.zeros((1, 128), jnp.float32))
-        first.append(jnp.concatenate(rows + rows, axis=0))
-    send(jnp.int32(0), first)
+        arrive(jnp.int32(0), p, jnp.concatenate(rows + rows, axis=0))
+    send(jnp.int32(0))
 
     inputs[3].wait()
     inputs[4].wait()
@@ -451,7 +455,7 @@
         def _():
             for copy in far_copies[1:]:
                 copy.wait_recv()
-            slots = pltpu.make_async_copy(far_slots_in, far_slots, input_sem.at[5])
+            slots = pltpu.make_async_copy(far_slots_in, far_slots, input_sem.at[7])
             slots.start()
             slots.wait()
             for d in range(1, n_tm):
@@ -493,23 +497,35 @@
                 heat = jnp.concatenate([heat, jnp.zeros((4, 128), jnp.float32)], axis=0)
                 base[p] = pair + retained[p] * state[p] + heat
 
-        @pl.when(is_far & (step >= AHEAD))
-        def _():
-            listed_by_partner(step - 1)
-
         for side in range(2):
 
             @pl.when(near(step, side))
             def _():
+                halo_copy(slot, side).wait_send()
+
+        @pl.when(is_far & fields_go(step))
+        def _():
+            field_copy(step).wait_send()
+
+        @pl.when(is_relay & fields_go(step))
+        def _():
+            relay_copy(step).wait_send()
+
+        @pl.when(is_far & (step >= AHEAD))
+        def _():
+            listed_by_partner(step - 1)
+
+        for side in (1 - cross, cross):
+
+            @pl.when(near(step, side))
+            def _(side=side):
                 halo_copy(slot, 1 - side).wait_recv()
 
-        for side in range(2):
             for q in range(HALO // 2):
                 value = inbox[slot, side, pl.ds(4 * q, 4), :]
                 n = NBLK + HALO * side + 2 * q
                 parts[n], parts[n + 1] = four_rows(value)
 
-        values = []
         for g in range(GROUPS):
             picked = []
             for b in range(4 * g, 4 * g + 4):
@@ -530,26 +546,13 @@
             )
             for h, pair in enumerate(on_diagonal(product)):
                 total = base[2 * g + h] + pair
-                values.append(total + pltpu.roll(total, 4, 0))
-                reached[2 * g + h] = values[-1]
-
-        for side in range(2):
-
-            @pl.when(near(step, side))
-            def _():
-                halo_copy(slot, side).wait_send()
-
-        @pl.when(is_far & fields_go(step))
-        def _():
-            field_copy(step).wait_send()
-
-        @pl.when(is_relay & fields_go(step))
-        def _():
-            relay_copy(step).wait_send()
+                value = total + pltpu.roll(total, 4, 0)
+                reached[2 * g + h] = value
+                arrive(step + 1, 2 * g + h, value)
 
         @pl.when(step < STEPS - 1)
         def _():
-            send(step + 1, [reached[p] for p in range(PAIRS)])
+            send(step + 1)
 
         return carry
 
@@ -574,13 +577,15 @@
 def body(n_tm, n_space, coupling, retain, sources, initial_guess, start_field, block_columns, send_lists):
     count = retain.shape[0]
     f32, bf16 = jnp.float32, jnp.bfloat16
-    smem, vmem = (pl.BlockSpec(memory_space=space) for space in (pltpu.SMEM, pltpu.VMEM))
+    vmem = pl.BlockSpec(memory_space=pltpu.VMEM)
     return pl.pallas_call(
         functools.partial(kernel, n_tm, n_space),
         out_shape=(jax.ShapeDtypeStruct((C_DEV, count), f32),) * 2,
-        in_specs=[smem, smem] + [pl.BlockSpec(memory_space=pl.ANY)] * 6,
+        in_specs=[pl.BlockSpec(memory_space=pl.ANY)] * 7,
         out_specs=(vmem, vmem),
         scratch_shapes=[
+            pltpu.SMEM((STENCIL - 1, NBLK), jnp.int32),
+            pltpu.SMEM((2, HALO), jnp.int32),
             pltpu.VMEM((PAIRS, 128), f32),
             pltpu.VMEM((C_DEV * CF, count), f32),
             pltpu.VMEM((C_DEV, count), f32),
@@ -620,7 +625,7 @@
             pltpu.VMEM((STEPS, 32, 128), f32),
             pltpu.VMEM((NBLK + 2 * HALO, 8, 128), f32),
             pltpu.SemaphoreType.DMA((STENCIL,)),
-            pltpu.SemaphoreType.DMA((6,)),
+            pltpu.SemaphoreType.DMA((8,)),
             pltpu.SemaphoreType.DMA((2, 2)),
             pltpu.SemaphoreType.DMA((2, 2)),
             pltpu.SemaphoreType.DMA((7,)),
@@ -638,7 +643,6 @@
             collective_id=0, has_side_effects=True, vmem_limit_bytes=60 * 2**20
         ),
     )(
-        block_columns.T,
         send_lists,
         coupling,
         retain.reshape(PAIRS, 128),

time: 94.4 us -> 93.5 us (level)
  no operation moved by 1% of the time
where the time goes in v5:
time: 93.5 us; the launch traced here: 92.5 us
  Pallas kernels  89.1 us (95%)
  local copies, waits for them, and re-layouts  2.76 us (3%)
    pallas_call x1, Pallas kernels, body(): pl.pallas_call(functools.partial(kernel, n_tm, n_space), out_shape=(jax.S...  89.1 us
    unnamed x2, local copies, waits for them, and re-layouts  2.76 us

profile of v5, /device:TPU:71, one launch (start us, length us, event | category | flops | bytes accessed | tf_op | source)
XLA Modules:
  0.0 92.5 jit_solution(4208546621140376016)
XLA Ops:
  0.6 89.1 %shard_map.86 = (f32[3,2048]{1,0:T(4,128)}, f32[3,2048]{1,0:T(4,128)}) custom-call(s32[2,16]{1,0:T(2,128)} %lists_hbm.1, f32[448,2048]{1,0:T(8,128)} %coupling_hbm.1, f32[16,128]{1,0:T(8,128)} %bitcast.3, f32[12,2048]{1,0:T(8,128)} %sources_hbm.1, f32[3,2048]{1,0:T(4,128)} %guess_hbm.1, f32[16,128]{1,0:T(8,128)} %bitcast.4, s32[6,32]{1,0:T(8,128)} %bitcast.5), custom_call_target="tpu_custom_call" | custom-call | tf_op jit(solution)/shard_map/pallas_call | solution.py:581
  89.7 1.4 %copy.11 = f32[3,2048]{1,0:T(4,128)} copy(f32[3,2048]{1,0:T(4,128)} %get-tuple-element.4) | data formatting | bytes 49152
  91.1 1.4 %copy.12 = f32[3,2048]{1,0:T(4,128)} copy(f32[3,2048]{1,0:T(4,128)} %get-tuple-element.5) | data formatting | bytes 49152

commit v6 on v5

--- a/solution.py
+++ b/solution.py
@@ -20,7 +20,7 @@
 REST = (STENCIL - 1) * BS
 ROW = 8
 SPREAD = 1
-AHEAD = 4
+AHEAD = 3
 MESH = pl.DeviceIdType.MESH
 
 

time: 93.5 us -> 93.3 us (level)
  no operation moved by 1% of the time
where the time goes in v6:
time: 93.3 us; the launch traced here: 91.9 us
  Pallas kernels  88.5 us (95%)
  local copies, waits for them, and re-layouts  2.76 us (3%)
    pallas_call x1, Pallas kernels, body(): pl.pallas_call(functools.partial(kernel, n_tm, n_space), out_shape=(jax.S...  88.5 us
    unnamed x2, local copies, waits for them, and re-layouts  2.76 us

profile of v6, /device:TPU:71, one launch (start us, length us, event | category | flops | bytes accessed | tf_op | source)
XLA Modules:
  0.0 91.9 jit_solution(6350139902964495026)
XLA Ops:
  0.6 88.5 %shard_map.86 = (f32[3,2048]{1,0:T(4,128)}, f32[3,2048]{1,0:T(4,128)}) custom-call(s32[2,16]{1,0:T(2,128)} %lists_hbm.1, f32[448,2048]{1,0:T(8,128)} %coupling_hbm.1, f32[16,128]{1,0:T(8,128)} %bitcast.3, f32[12,2048]{1,0:T(8,128)} %sources_hbm.1, f32[3,2048]{1,0:T(4,128)} %guess_hbm.1, f32[16,128]{1,0:T(8,128)} %bitcast.4, s32[6,32]{1,0:T(8,128)} %bitcast.5), custom_call_target="tpu_custom_call" | custom-call | tf_op jit(solution)/shard_map/pallas_call | solution.py:581
  89.1 1.4 %copy.11 = f32[3,2048]{1,0:T(4,128)} copy(f32[3,2048]{1,0:T(4,128)} %get-tuple-element.4) | data formatting | bytes 49152
  90.5 1.4 %copy.12 = f32[3,2048]{1,0:T(4,128)} copy(f32[3,2048]{1,0:T(4,128)} %get-tuple-element.5) | data formatting | bytes 49152

commit v7 on v6

--- a/solution.py
+++ b/solution.py
@@ -130,6 +130,9 @@
         return pl.ds(128 * p, 128)
 
     inbox[...] = jnp.zeros_like(inbox)
+    outbox[...] = jnp.zeros_like(outbox)
+    for step in range(STEPS):
+        relay_in[step, pl.ds(24, 8), :] = jnp.zeros((8, 128), jnp.float32)
     barrier = pltpu.get_barrier_semaphore()
     for other in (before[1], before[2], after[1], after[2]):
         pl.semaphore_signal(barrier, inc=1, device_id={"tm": other}, device_id_type=MESH)
@@ -183,8 +186,8 @@
 
     def halo_copy(slot, side):
         return pltpu.make_async_remote_copy(
-            src_ref=outbox.at[slot, side],
-            dst_ref=inbox.at[slot, 1 - side],
+            src_ref=outbox.at[slot, side, pl.ds(0, 24), :],
+            dst_ref=inbox.at[slot, 1 - side, pl.ds(0, 24), :],
             send_sem=send_sem.at[slot, side],
             recv_sem=recv_sem.at[slot, 1 - side],
             device_id={"space": space + 2 * side - 1},
@@ -243,8 +246,8 @@
     def relay_copy(step):
         slot = lax.rem(step, 2)
         return pltpu.make_async_remote_copy(
-            src_ref=outbox.at[slot, upper_half],
-            dst_ref=relay_in.at[step],
+            src_ref=outbox.at[slot, upper_half, pl.ds(0, 24), :],
+            dst_ref=relay_in.at[step, pl.ds(0, 24), :],
             send_sem=relay_send.at[slot],
             recv_sem=relay_recv.at[step],
             device_id={"space": second},
@@ -286,7 +289,7 @@
         for side in (cross, 1 - cross):
             for q in range(HALO // 2):
                 pair = jnp.where(low, doubled[lists[side, 2 * q]], doubled[lists[side, 2 * q + 1]])
-                outbox[slot, side, pl.ds(4 * q, 4), :] = pair[:4]
+                outbox[slot, side, pl.ds(3 * q, 3), :] = pair[:3]
 
             @pl.when(near(step, side))
             def _():
@@ -376,9 +379,9 @@
             far_parts[2 * p], far_parts[2 * p + 1] = four_rows(far_in[step, pl.ds(4 * p, 4), :])
         for q in range(HALO // 2):
             at = NBLK + HALO * upper_half + 2 * q
-            far_parts[at], far_parts[at + 1] = four_rows(relay_in[step, pl.ds(4 * q, 4), :])
+            far_parts[at], far_parts[at + 1] = four_rows(relay_in[step, pl.ds(3 * q, 4), :])
             at = NBLK + HALO * (1 - upper_half) + 2 * q
-            far_parts[at], far_parts[at + 1] = four_rows(outbox[slot, upper_half, pl.ds(4 * q, 4), :])
+            far_parts[at], far_parts[at + 1] = four_rows(outbox[slot, upper_half, pl.ds(3 * q, 4), :])
         begins = jnp.where(lax.rem(step + 1, CF) == 0, 4 - C_DEV * tm - (step + 1) // CF, -1)
         for g in range(HALO // 4):
             picked, firsts = [], []
@@ -406,7 +409,7 @@
                 total = pair + far_cells[pl.ds(q, 1), :] * now + heat
                 value = total + pltpu.roll(total, 4, 0)
                 value = jnp.where(field == begins, far_cells[pl.ds(8 + q, 1), :], value)
-                inbox[1 - slot, upper_half, pl.ds(4 * q, 4), :] = value[:4]
+                inbox[1 - slot, upper_half, pl.ds(3 * q, 3), :] = value[:3]
 
     def one_step(step, carry):
         slot = lax.rem(step, 2)
@@ -522,7 +525,7 @@
                 halo_copy(slot, 1 - side).wait_recv()
 
             for q in range(HALO // 2):
-                value = inbox[slot, side, pl.ds(4 * q, 4), :]
+                value = inbox[slot, side, pl.ds(3 * q, 4), :]
                 n = NBLK + HALO * side + 2 * q
                 parts[n], parts[n + 1] = four_rows(value)
 

time: 93.3 us -> 92 us (0.986); the launches traced: 91.9 us -> 91.7 us
  no operation moved by 1% of the time
where the time goes in v7:
time: 92 us; the launch traced here: 91.7 us
  Pallas kernels  88.3 us (96%)
  local copies, waits for them, and re-layouts  2.76 us (3%)
    pallas_call x1, Pallas kernels, body(): pl.pallas_call(functools.partial(kernel, n_tm, n_space), out_shape=(jax.S...  88.3 us
    unnamed x2, local copies, waits for them, and re-layouts  2.76 us

profile of v7, /device:TPU:71, one launch (start us, length us, event | category | flops | bytes accessed | tf_op | source)
XLA Modules:
  0.0 91.7 jit_solution(3224865367428973573)
XLA Ops:
  0.6 88.3 %shard_map.86 = (f32[3,2048]{1,0:T(4,128)}, f32[3,2048]{1,0:T(4,128)}) custom-call(s32[2,16]{1,0:T(2,128)} %lists_hbm.1, f32[448,2048]{1,0:T(8,128)} %coupling_hbm.1, f32[16,128]{1,0:T(8,128)} %bitcast.3, f32[12,2048]{1,0:T(8,128)} %sources_hbm.1, f32[3,2048]{1,0:T(4,128)} %guess_hbm.1, f32[16,128]{1,0:T(8,128)} %bitcast.4, s32[6,32]{1,0:T(8,128)} %bitcast.5), custom_call_target="tpu_custom_call" | custom-call | tf_op jit(solution)/shard_map/pallas_call | solution.py:584
  88.9 1.4 %copy.11 = f32[3,2048]{1,0:T(4,128)} copy(f32[3,2048]{1,0:T(4,128)} %get-tuple-element.4) | data formatting | bytes 49152
  90.3 1.4 %copy.12 = f32[3,2048]{1,0:T(4,128)} copy(f32[3,2048]{1,0:T(4,128)} %get-tuple-element.5) | data formatting | bytes 49152
